TPU v7x, 128 devices: a whole 4x4x4 slice. The times are simulated.
128 devices in a mesh: nodes: 16 (over x, z_hi, core), feat: 8 (over y, z_lo).
Axes of the slice: x: 4, y: 4, z: 4 (z_hi: 2, z_lo: 2; z = z_hi * 2 + z_lo), core: 2. Of those that a mesh axis runs over, the one named last changes fastest.
Arguments:
- feats: bfloat16 [128, 262144], P('feat', 'nodes'), may hold values from -6 to 6
- tile_src: int32 [2048, 20], P(('nodes', 'feat')), may hold values from 0 to 2047, as said below
- tile_weight: bfloat16 [2048, 20, 128, 128], P(('nodes', 'feat')), as said below
- w_one: bfloat16 [128, 512], replicated, may hold values from -0.5 to 0.5
- b_one: float32 [256], replicated, may hold values from -3 to 3
- w_two: bfloat16 [512, 256], replicated, may hold values from -0.375 to 0.375
- b_two: float32 [256], replicated, may hold values from -3 to 3
- cotangent: bfloat16 [262144, 256], P(('nodes', 'feat')), may hold values from -0.01171875 to 0.01171875
Outputs:
- layer_out: bfloat16 [262144, 256], P(('nodes', 'feat'))
- grad_w_two: float32 [512, 256], replicated
- grad_b_two: float32 [256], replicated
Inputs may be any that keep to these rules, and one draw needn't show every extreme that they name: `tile_src`: the 20 source blocks of a block are distinct and lie among the blocks of its own device and of the devices just before and after it in node order, the last device followed by the first; a device holds 16 consecutive blocks. `tile_weight`: each destination node draws d neighbour samples, d from 15 to 25, with replacement among the 2560 source nodes of its block's tiles; each sample adds 1 / d (rounded to bfloat16 with its count) to that source's entry in the node's row, and all other entries are zero.
All inputs are finite; a program needn't handle non-finite values.
Results may differ from a plain program's by a relative error of at most 0.0048.
Values may be sent and summed in bfloat16 or wider, within the bound.
A program may use at most 128 MiB of HBM per device.

v0:
```python
import jax
import jax.numpy as jnp
from jax import lax
from jax.sharding import PartitionSpec as P


def extended_2(cells, sides, width):
    for axis, dim in sides:
        count = lax.axis_size(axis)
        head = lax.slice_in_dim(cells, 0, width, axis=dim)
        tail = lax.slice_in_dim(cells, cells.shape[dim] - width, cells.shape[dim], axis=dim)
        cells = jnp.concatenate(
            [
                lax.ppermute(tail, axis, [(i, (i + 1) % count) for i in range(count)]),
                cells,
                lax.ppermute(head, axis, [((i + 1) % count, i) for i in range(count)]),
            ],
            axis=dim,
        )
    return cells


def aggregate(extended, local_src, tile_weight):
    tile = tile_weight.shape[-1]
    width = extended.shape[1]
    blocks = extended.reshape(-1, tile, width)
    picked = blocks[local_src]
    summed = jnp.einsum("bkij,bkjc->bic", tile_weight, picked, preferred_element_type=jnp.float32)
    return summed.reshape(-1, width)


def per_device(feats, tile_src, tile_weight, w_one, b_one, w_two, b_two, cotangent):
    rows = cotangent.shape[0]
    hidden = w_two.shape[1]
    width = feats.shape[0]
    w_part = lax.dynamic_slice_in_dim(w_one, lax.axis_index("feat") * width, width, 0)
    proj = lax.psum_scatter(
        lax.dot_general(
            feats, w_part, (((0,), (0,)), ((), ())), preferred_element_type=jnp.float32
        ),
        "feat",
        scatter_dimension=0,
        tiled=True,
    )
    ranked = lax.axis_index(("nodes", "feat"))
    block_count = tile_src.shape[0]
    total_blocks = block_count * lax.axis_size(("nodes", "feat"))
    local_src = (tile_src - (ranked - 1) * block_count) % total_blocks
    neigh_one = proj[:, hidden:].astype(jnp.bfloat16)
    neigh_ext = extended_2(neigh_one, ((("nodes", "feat"), 0),), rows)
    hidden_one = jax.nn.relu(
        proj[:, :hidden] + aggregate(neigh_ext, local_src, tile_weight) + b_one
    ).astype(jnp.bfloat16)
    hidden_ext = extended_2(hidden_one, ((("nodes", "feat"), 0),), rows)
    mixed = aggregate(hidden_ext, local_src, tile_weight).astype(jnp.bfloat16)
    both = jnp.concatenate([hidden_one, mixed], axis=1)
    layer_out = (jnp.dot(both, w_two, preferred_element_type=jnp.float32) + b_two).astype(
        jnp.bfloat16
    )
    local_w = lax.dot_general(
        both, cotangent, (((0,), (0,)), ((), ())), preferred_element_type=jnp.float32
    )
    local_b = jnp.sum(cotangent.astype(jnp.float32), axis=0)
    grad_w_two, grad_b_two = lax.psum((local_w, local_b), ("nodes", "feat"))
    return (layer_out, grad_w_two, grad_b_two)


def solution(mesh):
    return jax.shard_map(
        per_device,
        mesh=mesh,
        in_specs=(
            P("feat", "nodes"),
            P(("nodes", "feat"), None),
            P(("nodes", "feat"), None, None, None),
            P(),
            P(),
            P(),
            P(),
            P(("nodes", "feat"), None),
        ),
        out_specs=(P(("nodes", "feat"), None), P(), P()),
        check_vma=False,
    )
```

profile of v0, /device:TPU:1, one launch (start us, length us, event | category | flops | bytes accessed | tf_op | source)
XLA Modules:
  0.0 1040.7 jit_solution(8933181658211576736)
XLA Ops:
  7.2 0.0 copy-start
  7.2 0.0 reduce-scatter.2.cloned.1.call-start
  7.2 1.0 copy-done
  8.2 13.9 %convolution_bitcast_fusion = f32[16384,512]{0,1:T(8,128)} fusion(bf16[16,16384]{1,0:T(8,128)(2,1)S(1)} %copy-done, bf16[128,512]{1,0:T(8,128)(2,1)} %param.11, s32[]{:T(128)S(6)} %select_n.14), kind=kOutput, calls=%fused_computation.2 | convolution fusion | flops 268435456 | bytes 34095108 | tf_op jit(solution)/shard_map/dot_general | solution.py:38
  22.1 0.0 copy-start.6
  22.1 0.0 reduce-scatter.2.cloned.1.call-update
  22.1 0.0 all-reduce.2.cloned.1.call-start
  22.2 644.5 %reduce-scatter.2.cloned.1.call-done = f32[2048,512]{0,1:T(8,128)} async-done(((f32[16384,512]{0,1:T(8,128)}), f32[2048,512]{0,1:T(8,128)}) %reduce-scatter.2.cloned.1.call-update) | async-done | bytes 4194320 | tf_op jit(solution)/shard_map/reduce_scatter | solution.py:37
  666.6 1.7 slice.23
  668.4 0.1 collective-permute-start
  668.5 3.8 collective-permute-start.1
  672.3 0.0 copy-done.6
  672.3 0.1 reshape.24
  672.4 40.5 %collective-permute-done = bf16[2048,256]{0,1:T(8,128)(2,1)S(1)} collective-permute-done((bf16[2048,256]{0,1:T(8,128)(2,1)S(1)}, bf16[2048,256]{0,1:T(8,128)(2,1)S(1)}, u32[]{:S(2)}, u32[]{:S(2)}) %collective-permute-start) | collective-permute-done | bytes 1048608 | tf_op jit(solution)/shard_map/ppermute | solution.py:14
  712.9 0.0 collective-permute-done.1
  712.9 1.7 pad_maximum_fusion
  714.6 3.2 copy.21
  717.8 11.3 %gather_fusion = bf16[320,128,256]{2,1,0:T(8,128)(2,1)} fusion(bf16[48,128,256]{2,1,0:T(8,128)(2,1)S(1)} %bitcast.26, s32[1024]{0:T(1024)S(1)} %pad_clamp_fusion), kind=kCustom, calls=%fused_computation | custom fusion | bytes 41944320 | tf_op jit(solution)/shard_map/gather | solution.py:27
  729.1 12.8 %fusion.10 = f32[16,256,128,1]{1,2,3,0:T(8,128)S(1)} fusion(bf16[16,20,128,128]{3,2,1,0:T(8,128)(2,1)} %param.10, bf16[16,20,128,256]{3,2,1,0:T(8,128)(2,1)} %bitcast.28), kind=kOutput, calls=%fused_computation.26 | convolution fusion | flops 2684354560 | bytes 33554432 | tf_op jit(solution)/shard_map/bkij,bkjc->bic/dot_general | solution.py:28
  742.0 0.0 copy-start.7
  742.0 0.0 copy-start.4
  742.0 1.9 copy.22
  743.9 0.0 copy-done.7
  743.9 2.5 fusion.3
  746.4 0.0 copy-start.2
  746.4 2.3 collective-permute-start.2
  748.7 3.8 collective-permute-start.3
  752.4 0.0 copy-done.4
  752.4 0.3 convert_reduce_fusion
  752.7 101.9 %psum.15 = f32[256]{0:T(256)} all-reduce(f32[256]{0:T(256)S(1)} %convert_reduce_fusion), channel_id=1, replica_groups=mesh['nodes'=16,'feat'=8] {'nodes','feat'}, use_global_device_ids=true, to_apply=%region_3.4 | all-reduce | flops 256 | bytes 2048 | tf_op jit(solution)/shard_map/psum | solution.py:64
  854.6 0.0 collective-permute-done.2
  854.6 0.0 collective-permute-done.3
  854.6 0.0 copy-done.2
  854.6 2.8 pad_maximum_fusion.1
  857.4 3.2 copy.23
  860.6 11.3 %gather_fusion.1 = bf16[320,128,256]{2,1,0:T(8,128)(2,1)} fusion(bf16[48,128,256]{2,1,0:T(8,128)(2,1)S(1)} %bitcast.25, s32[1024]{0:T(1024)S(1)} %pad_clamp_fusion), kind=kCustom, calls=%fused_computation.1 | custom fusion | bytes 41944320 | tf_op jit(solution)/shard_map/gather | solution.py:27
  871.9 13.0 %bitcast_convert_fusion = bf16[16,256,128]{1,2,0:T(8,128)(2,1)S(1)} fusion(bf16[16,20,128,128]{3,2,1,0:T(8,128)(2,1)} %param.10, bf16[16,20,128,256]{3,2,1,0:T(8,128)(2,1)} %bitcast.27), kind=kOutput, calls=%fused_computation.13 | convolution fusion | flops 2684878848 | bytes 32505856 | tf_op jit(solution)/shard_map/bkij,bkjc->bic/dot_general | solution.py:28
  884.9 1.4 copy.24
  886.3 0.0 copy-done.3
  886.3 0.0 copy-done.5
  886.4 2.8 fusion.4
  889.1 0.0 all-reduce.2.cloned.1.call-update
  889.2 0.0 copy-done.8
  889.2 0.0 copy-done.9
  889.2 3.0 fusion
  892.2 139.8 %all-reduce.2.cloned.1.call-done = f32[512,256]{1,0:T(8,128)} async-done(((f32[512,256]{1,0:T(8,128)}), f32[512,256]{1,0:T(8,128)}) %all-reduce.2.cloned.1.call-update) | async-done | bytes 524304 | tf_op jit(solution)/shard_map/psum | solution.py:64
  1032.0 1.9 copy.26
  1033.9 0.0 copy-done.1
  (7 shorter events, 0.0 us)
Async XLA Ops:
  7.2 1.1 copy-start
  7.2 659.5 %reduce-scatter.2.cloned.1.call-start = ((), (), s32[]{:S(2)}) async-start(), calls=%async_computation.1 | async-start | bytes 37748736 | tf_op jit(solution)/shard_map/reduce_scatter | solution.py:37
  22.1 650.2 %copy-start.6 = (s32[16,20]{1,0:T(8,128)S(1)}, s32[16,20]{1,0:T(8,128)}, u32[]{:S(2)}) copy-start(s32[16,20]{1,0:T(8,128)} %param.9) | copy-start | bytes 3844
  22.1 1009.9 %all-reduce.2.cloned.1.call-start = ((), (), s32[]{:S(2)}) async-start(), calls=%async_computation.2 | async-start | bytes 1048576 | tf_op jit(solution)/shard_map/psum | solution.py:64
  668.4 44.5 %collective-permute-start = (bf16[2048,256]{0,1:T(8,128)(2,1)S(1)}, bf16[2048,256]{0,1:T(8,128)(2,1)S(1)}, u32[]{:S(2)}, u32[]{:S(2)}) collective-permute-start(bf16[2048,256]{0,1:T(8,128)(2,1)S(1)} %slice.23), channel_id=1, source_target_pairs={{0,1},{1,2},{2,3},{3,4},{4,5},{5,6},{6,7},{7,8},{8,9},{9,10},{10,1... | collective-permute-start | bytes 3145736 | tf_op jit(solution)/shard_map/ppermute | solution.py:14
  668.5 44.4 %collective-permute-start.1 = (bf16[2048,256]{0,1:T(8,128)(2,1)S(1)}, bf16[2048,256]{0,1:T(8,128)(2,1)S(1)}, u32[]{:S(2)}, u32[]{:S(2)}) collective-permute-start(bf16[2048,256]{0,1:T(8,128)(2,1)S(1)} %slice.23), channel_id=1, source_target_pairs={{1,0},{2,1},{3,2},{4,3},{5,4},{6,5},{7,6},{8,7},{9,8},{10,9},{11,1... | collective-permute-start | bytes 3145736 | tf_op jit(solution)/shard_map/ppermute | solution.py:16
  742.0 1.9 copy-start.7
  742.0 10.4 %copy-start.4 = (bf16[2048,256]{1,0:T(8,128)(2,1)S(1)}, bf16[2048,256]{1,0:T(8,128)(2,1)}, u32[]{:S(2)}) copy-start(bf16[2048,256]{1,0:T(8,128)(2,1)} %param.15) | copy-start | bytes 3145732
  746.4 108.2 %copy-start.2 = (bf16[2048,256]{0,1:T(8,128)(2,1)}, bf16[2048,256]{0,1:T(8,128)(2,1)S(1)}, u32[]{:S(2)}) copy-start(bf16[2048,256]{0,1:T(8,128)(2,1)S(1)} %fusion.3) | copy-start | bytes 3145732
  746.4 108.2 %collective-permute-start.2 = (bf16[2048,256]{0,1:T(8,128)(2,1)S(1)}, bf16[2048,256]{0,1:T(8,128)(2,1)S(1)}, u32[]{:S(2)}, u32[]{:S(2)}) collective-permute-start(bf16[2048,256]{0,1:T(8,128)(2,1)S(1)} %fusion.3), channel_id=1, source_target_pairs={{0,1},{1,2},{2,3},{3,4},{4,5},{5,6},{6,7},{7,8},{8,9},{9,10},{10,1... | collective-permute-start | bytes 3145736 | tf_op jit(solution)/shard_map/ppermute | solution.py:14
  748.7 105.9 %collective-permute-start.3 = (bf16[2048,256]{0,1:T(8,128)(2,1)S(1)}, bf16[2048,256]{0,1:T(8,128)(2,1)}, u32[]{:S(2)}, u32[]{:S(2)}) collective-permute-start(bf16[2048,256]{0,1:T(8,128)(2,1)S(1)} %fusion.3), channel_id=1, source_target_pairs={{1,0},{2,1},{3,2},{4,3},{5,4},{6,5},{7,6},{8,7},{9,8},{10,9},{11,1... | collective-permute-start | bytes 3145736 | tf_op jit(solution)/shard_map/ppermute | solution.py:16
  871.9 14.4 %copy-start.3 = (bf16[2048,256]{0,1:T(8,128)(2,1)S(1)}, bf16[2048,256]{0,1:T(8,128)(2,1)}, u32[]{:S(2)}) copy-start(bf16[2048,256]{0,1:T(8,128)(2,1)} %copy-done.2) | copy-start | bytes 3145732
  871.9 14.4 %copy-start.5 = (bf16[2048,256]{1,0:T(8,128)(2,1)S(1)}, bf16[2048,256]{1,0:T(8,128)(2,1)}, u32[]{:S(2)}) copy-start(bf16[2048,256]{1,0:T(8,128)(2,1)} %param.15) | copy-start | bytes 3145732
  886.4 2.8 copy-start.8
  886.4 2.8 copy-start.9
  889.1 144.7 %copy-start.1 = (bf16[16,16384]{1,0:T(8,128)(2,1)S(1)}, bf16[16,16384]{1,0:T(8,128)(2,1)}, u32[]{:S(2)}) copy-start(bf16[16,16384]{1,0:T(8,128)(2,1)} %param.8) | copy-start | bytes 1572868
Sparse Core Ops, SparseCore 0:
  22.2 644.3 reduce-scatter.1
  889.3 142.6 all-reduce.1
where the time goes:
time: 1040 us
  waiting for transfers between devices  825 us (79%)
  blocking collectives  102 us (10%)
  matrix products  45.5 us (4%)
  local copies, waits for them, and re-layouts  37 us (4%)
  between operations  14.2 us (1%)
    reduce_scatter x1, waiting for transfers between devices, per_device(): lax.psum_scatter(lax.dot_general(feats, w_part, (((0,), (0,)), ((), ())),...  644 us
    psum x1, waiting for transfers between devices, per_device(): grad_w_two, grad_b_two = lax.psum((local_w, local_b), ('nodes', 'feat'))  140 us
    psum x1, blocking collectives, per_device(): grad_w_two, grad_b_two = lax.psum((local_w, local_b), ('nodes', 'feat'))  102 us
    ppermute x2, waiting for transfers between devices, extended_2(): lax.ppermute(tail, axis, [(i, (i + 1) % count) for i in range(count)])  40.5 us
    dot_general x2, matrix products, aggregate(): jnp.einsum('bkij,bkjc->bic', tile_weight, picked, preferred_element_type=...  25.8 us
    gather x2, local copies, waits for them, and re-layouts, aggregate(): picked = blocks[local_src]  22.6 us
  transfers between devices with their start and end apart: 6, of which 3 were waited for; matrix products, arithmetic and copies ran while one was open for 0% of the time, Pallas kernels for 0%

commit v1 on v0

v1 whole, which is shorter than its diff:
```python
import functools

import jax
import jax.numpy as jnp
from jax import lax
from jax.experimental import pallas as pl
from jax.experimental.pallas import tpu as pltpu
from jax.sharding import PartitionSpec as P

BF = jnp.bfloat16
F32 = jnp.float32
TILE = 128
MESH = pl.DeviceIdType.MESH


def remote(src, dst, send_sem, recv_sem, node, feat):
    return pltpu.make_async_remote_copy(
        src_ref=src, dst_ref=dst, send_sem=send_sem, recv_sem=recv_sem,
        device_id=(node, feat), device_id_type=MESH)


def drain(ref, sem):
    pltpu.make_async_copy(ref, ref, sem).wait()


def dot(a, b):
    return lax.dot_general(a, b, (((1,), (0,)), ((), ())), preferred_element_type=F32)


def kernel(nn, nf, nb, neigh, chunk_blocks,
           feats, src, a_hbm, w1_hbm, b1, w2_hbm, b2, cot_hbm,
           out_hbm, gw_hbm, gb_out,
           ft, fn, a_v, pn, hn, mn, cot_v, cot_t, w1_v, w2_v, out_v,
           gt, rt, st, qt, ct, gb, rb, sb, qb, cb, gfin,
           load_sem, fsend, fedge, frecv, psend, pbound, pfsend, pdir, pfwd,
           ars, arr, out_sem):
    fd = feats.shape[0]
    rows = nb * TILE
    hid = b1.shape[1]
    rp = hid // nn
    hb = rp // 2
    ch = chunk_blocks
    nch = nb // ch
    cr = ch * TILE
    n = lax.axis_index("nodes")
    f = lax.axis_index("feat")
    z = lax.rem(f, 2)
    n_next = lax.rem(n + 1, nn)
    n_prev = lax.rem(n + nn - 1, nn)

    loads = [
        pltpu.make_async_copy(w1_hbm, w1_v, load_sem.at[0]),
        pltpu.make_async_copy(cot_hbm, cot_v, load_sem.at[1]),
        pltpu.make_async_copy(a_hbm, a_v, load_sem.at[2]),
        pltpu.make_async_copy(w2_hbm, w2_v, load_sem.at[3]),
    ]
    for load in loads:
        load.start()

    barrier = pltpu.get_barrier_semaphore()

    def greet(node, feat):
        pl.semaphore_signal(barrier, inc=1, device_id=(node, feat), device_id_type=MESH)

    for d in range(1, nf):
        greet(n, lax.rem(f + d, nf))
    for d in range(1, nn):
        greet(lax.rem(n + d, nn), f)

    @pl.when(f == 0)
    def _():
        for g in range(nf):
            greet(n_prev, jnp.int32(g))

    @pl.when(f == nf - 1)
    def _():
        for g in range(nf):
            greet(n_next, jnp.int32(g))

    pl.semaphore_wait(barrier, nf + nn)

    def feat_copy(part, d):
        df = lax.rem(f + d, nf)
        j = lax.rem(df + nf + part - 1, nf)
        if part == 0:
            dn = jnp.where(df == 0, n_next, n)
        elif part == 2:
            dn = jnp.where(df == nf - 1, n_prev, n)
        else:
            dn = n
        s = feats.at[:, pl.ds(pl.multiple_of(j * rows, rows), rows)]
        t = ft.at[pl.ds(pl.multiple_of(f * fd, fd), fd), pl.ds(part * rows, rows)]
        return s, t, dn, df

    for part in (1, 0, 2):
        for d in range(1, nf):
            s, t, dn, df = feat_copy(part, d)
            remote(s, t, fsend.at[part], frecv.at[part], dn, df).start()
        s, t, dn, df = feat_copy(part, 0)
        if part == 1:
            pltpu.make_async_copy(s, t, frecv.at[part]).start()
        else:
            edge = f == (0 if part == 0 else nf - 1)

            @pl.when(edge)
            def _():
                remote(s, t, fedge.at[part], frecv.at[part], dn, df).start()

            @pl.when(jnp.logical_not(edge))
            def _():
                pltpu.make_async_copy(s, t, frecv.at[part]).start()

    loads[1].wait()

    def cot_step(i, acc):
        base = pl.multiple_of(i * TILE, TILE)
        c = cot_v[pl.ds(base, TILE), :]
        cot_t[:, pl.ds(base, TILE)] = c.T
        return acc + c.astype(F32).reshape(TILE // hb, hb, hid).sum(0)

    bias_part = lax.fori_loop(0, nb, cot_step, jnp.zeros((hb, hid), F32))

    def turn(part):
        drain(ft.at[:, pl.ds(part * rows, rows)], frecv.at[part])

        def step(i, carry):
            base = pl.multiple_of(part * rows + i * TILE, TILE)
            fn[part * nb + i] = ft[:, pl.ds(base, TILE)].T
            return carry

        lax.fori_loop(0, nb, step, 0, unroll=2)

    turn(1)
    turn(0)
    turn(2)
    loads[0].wait()
    loads[2].wait()

    first = (n * nf + f - 1) * nb
    total = nn * nf * nb

    def gather(table, b):
        acc = None
        for k in range(0, neigh, 2):
            picked = []
            for i in (k, k + 1):
                s = src[b, i] - first
                s = jnp.where(s >= total, s - total, s)
                s = jnp.where(s < 0, s + total, s)
                s = jnp.minimum(s, 3 * nb - 1)
                picked.append(table[s])
            p = dot(jnp.concatenate([a_v[b, k], a_v[b, k + 1]], axis=1),
                    jnp.concatenate(picked, axis=0))
            acc = p if acc is None else acc + p
        return acc

    partner = f + 1 - 2 * z
    bound_next = jnp.logical_and(f == nf - 1, lax.rem(n, 2) == 1)
    bound_prev = jnp.logical_and(f == 0, lax.rem(n, 2) == 0)
    out_base = z * (2 * nb)
    in_base = (2 - 2 * z) * nb

    def at_rows(base, c):
        return pn.at[pl.ds(base + c * ch, ch)]

    def one_chunk(c, carry):
        for i in range(ch):
            b = c * ch + i
            pn[nb + b] = gather(fn, b).astype(BF)
        own = at_rows(nb, c)
        remote(own, at_rows(out_base, c), psend.at[c], pdir.at[c], n, partner).start()

        @pl.when(bound_next)
        def _():
            remote(own, at_rows(0, c), pbound.at[c], pfwd.at[c], n_next, jnp.int32(0)).start()

        @pl.when(bound_prev)
        def _():
            remote(own, at_rows(2 * nb, c), pbound.at[c], pfwd.at[c], n_prev, jnp.int32(nf - 1)).start()

        return carry

    lax.fori_loop(0, nch, one_chunk, 0)

    skip = jnp.logical_or(jnp.logical_and(f == nf - 2, lax.rem(n, 2) == 1),
                          jnp.logical_and(f == 1, lax.rem(n, 2) == 0))
    fwd_f = lax.rem(f + jnp.where(z == 0, 2, nf - 2), nf)
    fwd_n = jnp.where(f == nf - 2, n_next, jnp.where(f == 1, n_prev, n))

    def forward(c):
        drain(at_rows(in_base, c), pdir.at[c])

        @pl.when(jnp.logical_not(skip))
        def _():
            remote(at_rows(in_base, c), at_rows(out_base, c), pfsend.at[c], pfwd.at[c], fwd_n, fwd_f).start()

    w_cat = jnp.concatenate([w1_v[:, :hid], w1_v[:, hid:]], axis=0)
    bias_one = b1[...]

    def hidden(base, count):
        def step(i, carry):
            at = pl.ds(base + i * 2, 2)
            fp = jnp.concatenate([fn[at], pn[at]], axis=2).reshape(2 * TILE, 2 * TILE)
            v = dot(fp, w_cat) + bias_one
            hn[at] = jnp.maximum(v, 0.0).astype(BF).reshape(2, TILE, hid)
            return carry

        lax.fori_loop(0, count // 2, step, 0)

    def reduce_nodes(g, r, k):
        for d in range(1, nn):
            dn = lax.rem(n + d, nn)
            remote(g.at[dn], r.at[n], ars.at[k], arr.at[k], dn, f).start()
        r[n] = g[n]

    def reduce_feat(g, r, s, q, k):
        drain(r.at[pl.ds(0, nn - 1)], arr.at[k])
        drain(g.at[pl.ds(0, nn - 1)], ars.at[k])
        tot = r[0]
        for i in range(1, nn):
            tot = tot + r[i]
        for t in range(4):
            i, j = t // 2, t % 2
            s[t, :, 0:TILE] = tot[i * hb:(i + 1) * hb, j * TILE:(j + 1) * TILE]
            if s.shape[2] > TILE:
                s[t, :, TILE:] = tot[rp:, :]
        for d in range(1, nf):
            df = lax.rem(f + d, nf)
            remote(s.at[df // 2], q.at[f], ars.at[k + 1], arr.at[k + 1], n, df).start()
        q[f] = s[f // 2]

    def back_feat(s, q, c, k):
        drain(q.at[pl.ds(0, nf - 1)], arr.at[k + 1])
        drain(q.at[pl.ds(0, nf - 1)], ars.at[k + 1])
        tot = q[0]
        for i in range(1, nf):
            tot = tot + q[i]
        if q.shape[2] > TILE:
            gb_out[...] = jnp.sum(tot[:, TILE:], axis=0, keepdims=True)
        y = f // 2
        c[y] = tot[:, 0:TILE]
        for d in (2, 4, 6):
            remote(c.at[y], c.at[y], ars.at[k + 2], arr.at[k + 2], n, lax.rem(f + d, nf)).start()

    def back_nodes(c, half, k):
        drain(c.at[pl.ds(0, 3)], arr.at[k + 2])
        drain(c.at[pl.ds(0, 3)], ars.at[k + 2])
        at = pl.ds(pl.multiple_of(half * hid + n * rp, rp), rp)
        gfin[at, :] = jnp.concatenate(
            [jnp.concatenate([c[0], c[1]], axis=1), jnp.concatenate([c[2], c[3]], axis=1)], axis=0)
        for d in range(1, nn):
            remote(gfin.at[at], gfin.at[at], ars.at[k + 3], arr.at[k + 3], lax.rem(n + d, nn), f).start()

    def finish(half, k):
        some = gfin.at[pl.ds(half * hid, (nn - 1) * rp)]
        drain(some, arr.at[k + 3])
        drain(some, ars.at[k + 3])
        at = pl.ds(half * hid, hid)
        return pltpu.make_async_copy(gfin.at[at], gw_hbm.at[at], load_sem.at[4 + half])

    forward(0)
    hidden(nb, nb)
    if nch > 1:
        forward(1)
    g_top = dot(cot_t[...], hn[nb:2 * nb].reshape(rows, hid)).T
    for i in range(nn):
        gt[i, 0:rp, :] = g_top[i * rp:(i + 1) * rp, :]
        gt[i, rp:, :] = bias_part
    reduce_nodes(gt, rt, 0)
    for c in range(2, nch):
        forward(c)
    hidden(in_base, nb)
    reduce_feat(gt, rt, st, qt, 0)

    def halo(c):
        drain(at_rows(out_base, c), pfwd.at[c])
        hidden(out_base + c * ch, ch)

    halo(0)
    back_feat(st, qt, ct, 0)
    if nch > 1:
        halo(1)
    back_nodes(ct, 0, 0)
    for c in range(2, nch):
        halo(c)

    loads[3].wait()
    bias_two = b2[...]

    def two_chunk(c, carry):
        for i in range(ch):
            b = c * ch + i
            at = pl.ds(pl.multiple_of(b * TILE, TILE), TILE)
            mn[at, :] = gather(hn, b).astype(BF)
        at = pl.ds(pl.multiple_of(c * cr, cr), cr)
        own = hn[pl.ds(nb + c * ch, ch)].reshape(cr, hid)
        both = jnp.concatenate([own, mn[at, :]], axis=1)
        out_v[at, :] = (dot(both, w2_v[...]) + bias_two).astype(BF)
        pltpu.make_async_copy(out_v.at[at], out_hbm.at[at], out_sem.at[c]).start()
        return carry

    lax.fori_loop(0, nch, two_chunk, 0)

    g_bot = dot(cot_t[...], mn[...]).T
    for i in range(nn):
        gb[i] = g_bot[i * rp:(i + 1) * rp, :]
    reduce_nodes(gb, rb, 4)
    top = finish(0, 0)
    top.start()

    for part in range(3):
        drain(ft.at[pl.ds(0, (nf - 1) * fd), pl.ds(0, rows)], fsend.at[part])

    @pl.when(f == 0)
    def _():
        drain(ft.at[pl.ds(0, fd), pl.ds(0, rows)], fedge.at[0])

    @pl.when(f == nf - 1)
    def _():
        drain(ft.at[pl.ds(0, fd), pl.ds(0, rows)], fedge.at[2])

    for c in range(nch):
        drain(at_rows(nb, c), psend.at[c])

        @pl.when(jnp.logical_or(bound_next, bound_prev))
        def _():
            drain(at_rows(nb, c), pbound.at[c])

        @pl.when(jnp.logical_not(skip))
        def _():
            drain(at_rows(in_base, c), pfsend.at[c])

    reduce_feat(gb, rb, sb, qb, 4)
    back_feat(sb, qb, cb, 4)
    back_nodes(cb, 1, 4)
    for c in range(nch):
        drain(out_v.at[pl.ds(c * cr, cr)], out_sem.at[c])
    bottom = finish(1, 4)
    bottom.start()
    top.wait()
    bottom.wait()


def per_device(nn, nf, feats, tile_src, tile_weight, w_one, b_one, w_two, b_two, cotangent):
    fd = feats.shape[0]
    nb, neigh = tile_src.shape
    rows = nb * TILE
    hid = b_one.shape[0]
    features = w_one.shape[0]
    rp = hid // nn
    hb = rp // 2
    ch = min(4, nb)
    nch = nb // ch
    anyspace = pl.BlockSpec(memory_space=pl.ANY)
    vm = pl.BlockSpec(memory_space=pltpu.VMEM)
    sm = pl.BlockSpec(memory_space=pltpu.SMEM)
    dma = pltpu.SemaphoreType.DMA
    out, gw, gb = pl.pallas_call(
        functools.partial(kernel, nn, nf, nb, neigh, ch),
        out_shape=(
            jax.ShapeDtypeStruct((rows, hid), BF),
            jax.ShapeDtypeStruct((2 * hid, hid), F32),
            jax.ShapeDtypeStruct((1, hid), F32),
        ),
        in_specs=[anyspace, sm, anyspace, anyspace, vm, anyspace, vm, anyspace],
        out_specs=(anyspace, anyspace, vm),
        scratch_shapes=[
            pltpu.VMEM((features, 3 * rows), BF),
            pltpu.VMEM((3 * nb, TILE, features), BF),
            pltpu.VMEM(tile_weight.shape, BF),
            pltpu.VMEM((3 * nb, TILE, features), BF),
            pltpu.VMEM((3 * nb, TILE, hid), BF),
            pltpu.VMEM((rows, hid), BF),
            pltpu.VMEM((rows, hid), BF),
            pltpu.VMEM((hid, rows), BF),
            pltpu.VMEM(w_one.shape, BF),
            pltpu.VMEM(w_two.shape, BF),
            pltpu.VMEM((rows, hid), BF),
            pltpu.VMEM((nn, rp + hb, hid), F32),
            pltpu.VMEM((nn, rp + hb, hid), F32),
            pltpu.VMEM((4, hb, TILE + hid), F32),
            pltpu.VMEM((nf, hb, TILE + hid), F32),
            pltpu.VMEM((4, hb, TILE), F32),
            pltpu.VMEM((nn, rp, hid), F32),
            pltpu.VMEM((nn, rp, hid), F32),
            pltpu.VMEM((4, hb, TILE), F32),
            pltpu.VMEM((nf, hb, TILE), F32),
            pltpu.VMEM((4, hb, TILE), F32),
            pltpu.VMEM((2 * hid, hid), F32),
            dma((6,)), dma((3,)), dma((3,)), dma((3,)),
            dma((nch,)), dma((nch,)), dma((nch,)), dma((nch,)), dma((nch,)),
            dma((8,)), dma((8,)), dma((nch,)),
        ],
        compiler_params=pltpu.CompilerParams(
            collective_id=0, has_side_effects=True, vmem_limit_bytes=56 * 2**20),
        name="sage",
    )(feats, tile_src, tile_weight, w_one, b_one.reshape(1, hid), w_two, b_two.reshape(1, hid), cotangent)
    return out, gw, gb.reshape(hid)


def solution(mesh):
    nn, nf = mesh.shape["nodes"], mesh.shape["feat"]
    return jax.shard_map(
        functools.partial(per_device, nn, nf),
        mesh=mesh,
        in_specs=(
            P("feat", "nodes"),
            P(("nodes", "feat"), None),
            P(("nodes", "feat"), None, None, None),
            P(),
            P(),
            P(),
            P(),
            P(("nodes", "feat"), None),
        ),
        out_specs=(P(("nodes", "feat"), None), P(), P()),
        check_vma=False,
    )
```

time: 1040 us -> 92.6 us (0.09)
  waiting for transfers between devices: 825 us -> 0 us
  blocking collectives: 102 us -> 0 us
  Pallas kernels: 0 us -> 86.3 us
  matrix products: 45.5 us -> 0 us
  local copies, waits for them, and re-layouts: 37 us -> 5.36 us
  between operations: 14.2 us -> 0.64 us
    reduce_scatter x1 -> x0, waiting for transfers between devices: 644 us -> none  [per_device(): lax.psum_scatter(lax.dot_general(feats, w_part, (((0,), (0,)), ((), ())),...]
    psum x1 -> x0, waiting for transfers between devices: 140 us -> none  [per_device(): grad_w_two, grad_b_two = lax.psum((local_w, local_b), ('nodes', 'feat'))]
    psum x1 -> x0, blocking collectives: 102 us -> none  [per_device(): grad_w_two, grad_b_two = lax.psum((local_w, local_b), ('nodes', 'feat'))]
    pallas_call x0 -> x1, Pallas kernels: none -> 86.3 us  [per_device(): pl.pallas_call(functools.partial(kernel, nn, nf, nb, neigh, ch), out_shap...]
    dot_general x5 -> x0, matrix products: 45.5 us -> none  [the longest x2 25.8 us: aggregate(): jnp.einsum('bkij,bkjc->bic', tile_weight, picked, preferred_element_type=...]
    ppermute x4 -> x0, waiting for transfers between devices: 40.5 us -> none  [the longest x2 40.5 us: extended_2(): lax.ppermute(tail, axis, [(i, (i + 1) % count) for i in range(count)])]
    gather x2 -> x0, local copies, waits for them, and re-layouts: 22.6 us -> none  [aggregate(): picked = blocks[local_src]]
  transfers between devices with their start and end apart: 6 -> 0, of which waited for: 3 -> 0; matrix products, arithmetic and copies ran while one was open for 0% -> 0% of each run, Pallas kernels for 0% -> 0%
where the time goes in v1:
time: 92.6 us; the launch traced here: 92.3 us
  Pallas kernels  86.3 us (93%)
  local copies, waits for them, and re-layouts  5.36 us (6%)
    pallas_call x1, Pallas kernels, per_device(): pl.pallas_call(functools.partial(kernel, nn, nf, nb, neigh, ch), out_shap...  86.3 us
    unnamed x3, local copies, waits for them, and re-layouts  5.36 us

profile of v1, /device:TPU:1, one launch (start us, length us, event | category | flops | bytes accessed | tf_op | source)
XLA Modules:
  0.0 92.3 jit_solution(9884959510727415157)
XLA Ops:
  0.6 86.3 %sage.1 = (bf16[2048,256]{1,0:T(8,128)(2,1)}, f32[512,256]{1,0:T(8,128)}, f32[1,256]{1,0:T(1,128)}) custom-call(bf16[16,16384]{1,0:T(8,128)(2,1)} %feats.1, s32[16,20]{1,0:T(8,128)} %src.1, bf16[16,20,128,128]{3,2,1,0:T(8,128)(2,1)} %a_hbm.1, bf16[128,512]{1,0:T(8,128)(2,1)} %w1_hbm.1, f32[1,256]{1,0:T(1,128)} %bitcast.3, bf16[512,256]{1,0:T(8,128)(2,1)} %w2_hbm.1, ...), custom_call_target="tpu_custom_call" | custom-call | tf_op jit(solution)/shard_map/sage/pallas_call | solution.py:358
  87.0 2.3 %copy.14 = bf16[2048,256]{1,0:T(8,128)(2,1)} copy(bf16[2048,256]{1,0:T(8,128)(2,1)} %get-tuple-element.12) | data formatting | bytes 2097152
  89.2 1.9 %copy.15 = f32[512,256]{1,0:T(8,128)} copy(f32[512,256]{1,0:T(8,128)} %get-tuple-element.13) | data formatting | bytes 1048576
  91.1 1.2 %copy.16 = f32[256]{0:T(256)} copy(f32[256]{0:T(256)} %bitcast.5) | data formatting | bytes 2048

commit v2 on v1

--- a/solution.py
+++ b/solution.py
@@ -27,18 +27,33 @@
     return lax.dot_general(a, b, (((1,), (0,)), ((), ())), preferred_element_type=F32)
 
 
+def tiles_of(nn):
+    tiles = max(nn // 2, 1)
+    columns = min(tiles, 2)
+    return tiles // columns, columns
+
+
+def hand_over(a, b, c, x, y, z, sem):
+    copies = [pltpu.make_async_copy(p, q, sem.at[i]) for i, (p, q) in enumerate(((a, x), (b, y), (c, z)))]
+    for copy in copies:
+        copy.start()
+    for copy in copies:
+        copy.wait()
+
+
 def kernel(nn, nf, nb, neigh, chunk_blocks,
            feats, src, a_hbm, w1_hbm, b1, w2_hbm, b2, cot_hbm,
            out_hbm, gw_hbm, gb_out,
            ft, fn, a_v, pn, hn, mn, cot_v, cot_t, w1_v, w2_v, out_v,
-           gt, rt, st, qt, ct, gb, rb, sb, qb, cb, gfin,
+           gt, rt, st, qt, ct, gb, rb, sb, qb, cb, gfin, gout, bslot,
            load_sem, fsend, fedge, frecv, psend, pbound, pfsend, pdir, pfwd,
            ars, arr, out_sem):
     fd = feats.shape[0]
     rows = nb * TILE
     hid = b1.shape[1]
-    rp = hid // nn
-    hb = rp // 2
+    fp = hid // nf
+    tr, tc = tiles_of(nn)
+    th, tw = fp // tr, hid // tc
     ch = chunk_blocks
     nch = nb // ch
     cr = ch * TILE
@@ -116,9 +131,9 @@
         base = pl.multiple_of(i * TILE, TILE)
         c = cot_v[pl.ds(base, TILE), :]
         cot_t[:, pl.ds(base, TILE)] = c.T
-        return acc + c.astype(F32).reshape(TILE // hb, hb, hid).sum(0)
-
-    bias_part = lax.fori_loop(0, nb, cot_step, jnp.zeros((hb, hid), F32))
+        return acc + c.astype(F32).reshape(TILE // th, th, hid).sum(0)
+
+    bias_part = lax.fori_loop(0, nb, cot_step, jnp.zeros((th, hid), F32))
 
     def turn(part):
         drain(ft.at[:, pl.ds(part * rows, rows)], frecv.at[part])
@@ -207,80 +222,86 @@
 
         lax.fori_loop(0, count // 2, step, 0)
 
-    def reduce_nodes(g, r, k):
+    def load_pieces(g, grad):
+        for i in range(nf):
+            g[i] = grad[i * fp:(i + 1) * fp, :].astype(BF)
+
+    def reduce_feat(g, r, k):
+        for d in range(1, nf):
+            df = lax.rem(f + d, nf)
+            remote(g.at[df], r.at[f], ars.at[k], arr.at[k], n, df).start()
+        r[f] = g[f]
+
+    def reduce_nodes(g, r, s, q, k, extra):
+        drain(r.at[pl.ds(0, nf - 1)], arr.at[k])
+        drain(g.at[pl.ds(0, nf - 1)], ars.at[k])
+        tot = r[0].astype(F32)
+        for i in range(1, nf):
+            tot = tot + r[i].astype(F32)
+        for t in range(tr * tc):
+            i, j = t // tc, t % tc
+            s[t, :, 0:tw] = tot[i * th:(i + 1) * th, j * tw:(j + 1) * tw]
+            if extra is not None:
+                s[t, :, tw:] = extra
         for d in range(1, nn):
             dn = lax.rem(n + d, nn)
-            remote(g.at[dn], r.at[n], ars.at[k], arr.at[k], dn, f).start()
-        r[n] = g[n]
-
-    def reduce_feat(g, r, s, q, k):
-        drain(r.at[pl.ds(0, nn - 1)], arr.at[k])
-        drain(g.at[pl.ds(0, nn - 1)], ars.at[k])
-        tot = r[0]
+            remote(s.at[dn // 2], q.at[n], ars.at[k + 1], arr.at[k + 1], dn, f).start()
+        q[n] = s[n // 2]
+
+    def back_nodes(q, c, k):
+        drain(q.at[pl.ds(0, nn - 1)], arr.at[k + 1])
+        drain(q.at[pl.ds(0, nn - 1)], ars.at[k + 1])
+        tot = q[0]
         for i in range(1, nn):
-            tot = tot + r[i]
-        for t in range(4):
-            i, j = t // 2, t % 2
-            s[t, :, 0:TILE] = tot[i * hb:(i + 1) * hb, j * TILE:(j + 1) * TILE]
-            if s.shape[2] > TILE:
-                s[t, :, TILE:] = tot[rp:, :]
+            tot = tot + q[i]
+        if q.shape[2] > tw:
+            bslot[f] = tot[:, tw:]
+        c[n // 2] = tot[:, 0:tw]
+        for d in range(2, nn, 2):
+            remote(c.at[n // 2], c.at[n // 2], ars.at[k + 2], arr.at[k + 2], lax.rem(n + d, nn), f).start()
+
+    def back_feat(c, half, k):
+        if nn > 2:
+            drain(c.at[pl.ds(0, nn // 2 - 1)], arr.at[k + 2])
+            drain(c.at[pl.ds(0, nn // 2 - 1)], ars.at[k + 2])
+        at = pl.ds(pl.multiple_of(half * hid + f * fp, fp), fp)
+        gfin[at, :] = jnp.concatenate(
+            [jnp.concatenate([c[i * tc + j] for j in range(tc)], axis=1) for i in range(tr)], axis=0).astype(BF)
         for d in range(1, nf):
             df = lax.rem(f + d, nf)
-            remote(s.at[df // 2], q.at[f], ars.at[k + 1], arr.at[k + 1], n, df).start()
-        q[f] = s[f // 2]
-
-    def back_feat(s, q, c, k):
-        drain(q.at[pl.ds(0, nf - 1)], arr.at[k + 1])
-        drain(q.at[pl.ds(0, nf - 1)], ars.at[k + 1])
-        tot = q[0]
-        for i in range(1, nf):
-            tot = tot + q[i]
-        if q.shape[2] > TILE:
-            gb_out[...] = jnp.sum(tot[:, TILE:], axis=0, keepdims=True)
-        y = f // 2
-        c[y] = tot[:, 0:TILE]
-        for d in (2, 4, 6):
-            remote(c.at[y], c.at[y], ars.at[k + 2], arr.at[k + 2], n, lax.rem(f + d, nf)).start()
-
-    def back_nodes(c, half, k):
-        drain(c.at[pl.ds(0, 3)], arr.at[k + 2])
-        drain(c.at[pl.ds(0, 3)], ars.at[k + 2])
-        at = pl.ds(pl.multiple_of(half * hid + n * rp, rp), rp)
-        gfin[at, :] = jnp.concatenate(
-            [jnp.concatenate([c[0], c[1]], axis=1), jnp.concatenate([c[2], c[3]], axis=1)], axis=0)
-        for d in range(1, nn):
-            remote(gfin.at[at], gfin.at[at], ars.at[k + 3], arr.at[k + 3], lax.rem(n + d, nn), f).start()
+            remote(gfin.at[at], gfin.at[at], ars.at[k + 3], arr.at[k + 3], n, df).start()
+            if half == 0:
+                remote(bslot.at[f], bslot.at[f], ars.at[8], arr.at[8], n, df).start()
 
     def finish(half, k):
-        some = gfin.at[pl.ds(half * hid, (nn - 1) * rp)]
+        some = gfin.at[pl.ds(half * hid, (nf - 1) * fp)]
         drain(some, arr.at[k + 3])
         drain(some, ars.at[k + 3])
         at = pl.ds(half * hid, hid)
-        return pltpu.make_async_copy(gfin.at[at], gw_hbm.at[at], load_sem.at[4 + half])
+        gout[at, :] = gfin[at, :].astype(F32)
+        return pltpu.make_async_copy(gout.at[at], gw_hbm.at[at], load_sem.at[4 + half])
 
     forward(0)
     hidden(nb, nb)
     if nch > 1:
         forward(1)
     g_top = dot(cot_t[...], hn[nb:2 * nb].reshape(rows, hid)).T
-    for i in range(nn):
-        gt[i, 0:rp, :] = g_top[i * rp:(i + 1) * rp, :]
-        gt[i, rp:, :] = bias_part
-    reduce_nodes(gt, rt, 0)
+    load_pieces(gt, g_top)
+    reduce_feat(gt, rt, 0)
     for c in range(2, nch):
         forward(c)
     hidden(in_base, nb)
-    reduce_feat(gt, rt, st, qt, 0)
+    reduce_nodes(gt, rt, st, qt, 0, bias_part)
 
     def halo(c):
         drain(at_rows(out_base, c), pfwd.at[c])
         hidden(out_base + c * ch, ch)
 
     halo(0)
-    back_feat(st, qt, ct, 0)
+    back_nodes(qt, ct, 0)
     if nch > 1:
         halo(1)
-    back_nodes(ct, 0, 0)
+    back_feat(ct, 0, 0)
     for c in range(2, nch):
         halo(c)
 
@@ -302,11 +323,16 @@
     lax.fori_loop(0, nch, two_chunk, 0)
 
     g_bot = dot(cot_t[...], mn[...]).T
-    for i in range(nn):
-        gb[i] = g_bot[i * rp:(i + 1) * rp, :]
-    reduce_nodes(gb, rb, 4)
+    load_pieces(gb, g_bot)
+    reduce_feat(gb, rb, 4)
     top = finish(0, 0)
     top.start()
+    drain(bslot.at[pl.ds(0, nf - 1)], arr.at[8])
+    drain(bslot.at[pl.ds(0, nf - 1)], ars.at[8])
+    col = bslot[0]
+    for i in range(1, nf):
+        col = col + bslot[i]
+    gb_out[...] = jnp.sum(col, axis=0, keepdims=True)
 
     for part in range(3):
         drain(ft.at[pl.ds(0, (nf - 1) * fd), pl.ds(0, rows)], fsend.at[part])
@@ -330,9 +356,9 @@
         def _():
             drain(at_rows(in_base, c), pfsend.at[c])
 
-    reduce_feat(gb, rb, sb, qb, 4)
-    back_feat(sb, qb, cb, 4)
-    back_nodes(cb, 1, 4)
+    reduce_nodes(gb, rb, sb, qb, 4, None)
+    back_nodes(qb, cb, 4)
+    back_feat(cb, 1, 4)
     for c in range(nch):
         drain(out_v.at[pl.ds(c * cr, cr)], out_sem.at[c])
     bottom = finish(1, 4)
@@ -347,8 +373,9 @@
     rows = nb * TILE
     hid = b_one.shape[0]
     features = w_one.shape[0]
-    rp = hid // nn
-    hb = rp // 2
+    fp = hid // nf
+    tr, tc = tiles_of(nn)
+    th, tw = fp // tr, hid // tc
     ch = min(4, nb)
     nch = nb // ch
     anyspace = pl.BlockSpec(memory_space=pl.ANY)
@@ -376,25 +403,35 @@
             pltpu.VMEM(w_one.shape, BF),
             pltpu.VMEM(w_two.shape, BF),
             pltpu.VMEM((rows, hid), BF),
-            pltpu.VMEM((nn, rp + hb, hid), F32),
-            pltpu.VMEM((nn, rp + hb, hid), F32),
-            pltpu.VMEM((4, hb, TILE + hid), F32),
-            pltpu.VMEM((nf, hb, TILE + hid), F32),
-            pltpu.VMEM((4, hb, TILE), F32),
-            pltpu.VMEM((nn, rp, hid), F32),
-            pltpu.VMEM((nn, rp, hid), F32),
-            pltpu.VMEM((4, hb, TILE), F32),
-            pltpu.VMEM((nf, hb, TILE), F32),
-            pltpu.VMEM((4, hb, TILE), F32),
+            pltpu.VMEM((nf, fp, hid), BF),
+            pltpu.VMEM((nf, fp, hid), BF),
+            pltpu.VMEM((tr * tc, th, tw + hid), F32),
+            pltpu.VMEM((nn, th, tw + hid), F32),
+            pltpu.VMEM((tr * tc, th, tw), F32),
+            pltpu.VMEM((nf, fp, hid), BF),
+            pltpu.VMEM((nf, fp, hid), BF),
+            pltpu.VMEM((tr * tc, th, tw), F32),
+            pltpu.VMEM((nn, th, tw), F32),
+            pltpu.VMEM((tr * tc, th, tw), F32),
+            pltpu.VMEM((2 * hid, hid), BF),
             pltpu.VMEM((2 * hid, hid), F32),
+            pltpu.VMEM((nf, th, hid), F32),
             dma((6,)), dma((3,)), dma((3,)), dma((3,)),
             dma((nch,)), dma((nch,)), dma((nch,)), dma((nch,)), dma((nch,)),
-            dma((8,)), dma((8,)), dma((nch,)),
+            dma((9,)), dma((9,)), dma((nch,)),
         ],
         compiler_params=pltpu.CompilerParams(
             collective_id=0, has_side_effects=True, vmem_limit_bytes=56 * 2**20),
         name="sage",
     )(feats, tile_src, tile_weight, w_one, b_one.reshape(1, hid), w_two, b_two.reshape(1, hid), cotangent)
+    out, gw, gb = pl.pallas_call(
+        hand_over,
+        out_shape=tuple(jax.ShapeDtypeStruct(v.shape, v.dtype) for v in (out, gw, gb)),
+        in_specs=[anyspace] * 3,
+        out_specs=(anyspace,) * 3,
+        scratch_shapes=[dma((3,))],
+        name="hand_over",
+    )(out, gw, gb)
     return out, gw, gb.reshape(hid)
 
 

time: 92.6 us -> 133 us (1.44)
  Pallas kernels: 86.3 us -> 132 us
  local copies, waits for them, and re-layouts: 5.36 us -> 0 us
    pallas_call x0 -> x1, Pallas kernels: none -> 48.8 us  [per_device(): pl.pallas_call(hand_over, out_shape=tuple((jax.ShapeDtypeStruct(v.shape,...]
    unnamed x3 -> x0, local copies, waits for them, and re-layouts: 5.36 us -> none
    pallas_call x1, Pallas kernels: 86.3 us -> 83.2 us  [per_device(): pl.pallas_call(functools.partial(kernel, nn, nf, nb, neigh, ch), out_shap...]
where the time goes in v2:
time: 133 us
  Pallas kernels  132 us (99%)
    pallas_call x1, Pallas kernels, per_device(): pl.pallas_call(functools.partial(kernel, nn, nf, nb, neigh, ch), out_shap...  83.2 us
    pallas_call x1, Pallas kernels, per_device(): pl.pallas_call(hand_over, out_shape=tuple((jax.ShapeDtypeStruct(v.shape,...  48.8 us

profile of v2, /device:TPU:1, one launch (start us, length us, event | category | flops | bytes accessed | tf_op | source)
XLA Modules:
  0.0 132.6 jit_solution(11772932964441737454)
XLA Ops:
  0.6 83.2 %sage.1 = (bf16[2048,256]{1,0:T(8,128)(2,1)}, f32[512,256]{1,0:T(8,128)}, f32[1,256]{1,0:T(1,128)}) custom-call(bf16[16,16384]{1,0:T(8,128)(2,1)} %feats.1, s32[16,20]{1,0:T(8,128)} %src.1, bf16[16,20,128,128]{3,2,1,0:T(8,128)(2,1)} %a_hbm.1, bf16[128,512]{1,0:T(8,128)(2,1)} %w1_hbm.1, f32[1,256]{1,0:T(1,128)} %bitcast.3, bf16[512,256]{1,0:T(8,128)(2,1)} %w2_hbm.1, ...), custom_call_target="tpu_custom_call" | custom-call | tf_op jit(solution)/shard_map/sage/pallas_call | solution.py:385
  83.8 48.8 %hand_over.1 = (bf16[2048,256]{1,0:T(8,128)(2,1)}, f32[512,256]{1,0:T(8,128)}, f32[1,256]{1,0:T(1,128)}) custom-call(bf16[2048,256]{1,0:T(8,128)(2,1)} %get-tuple-element.9.a, f32[512,256]{1,0:T(8,128)} %get-tuple-element.10.b, f32[1,256]{1,0:T(1,128)} %get-tuple-element.11.c), custom_call_target="tpu_custom_call" | custom-call | tf_op jit(solution)/shard_map/hand_over/pallas_call | solution.py:427

commit v3 on v1

--- a/solution.py
+++ b/solution.py
@@ -27,18 +27,26 @@
     return lax.dot_general(a, b, (((1,), (0,)), ((), ())), preferred_element_type=F32)
 
 
+def hand_over(out, gw, gb, out_copy, gw_wide, gb_sum):
+    out_copy[...] = out[...]
+    gw_wide[...] = gw[...].astype(F32)
+    tot = gb[0]
+    for i in range(1, gb.shape[0]):
+        tot = tot + gb[i]
+    gb_sum[...] = jnp.sum(tot, axis=0, keepdims=True)
+
+
 def kernel(nn, nf, nb, neigh, chunk_blocks,
            feats, src, a_hbm, w1_hbm, b1, w2_hbm, b2, cot_hbm,
-           out_hbm, gw_hbm, gb_out,
+           out_hbm, gw_hbm, gb_hbm,
            ft, fn, a_v, pn, hn, mn, cot_v, cot_t, w1_v, w2_v, out_v,
-           gt, rt, st, qt, ct, gb, rb, sb, qb, cb, gfin,
+           gt, rt, qt, gb, rb, qb, gfin, bslot,
            load_sem, fsend, fedge, frecv, psend, pbound, pfsend, pdir, pfwd,
            ars, arr, out_sem):
     fd = feats.shape[0]
     rows = nb * TILE
     hid = b1.shape[1]
     rp = hid // nn
-    hb = rp // 2
     ch = chunk_blocks
     nch = nb // ch
     cr = ch * TILE
@@ -116,9 +124,9 @@
         base = pl.multiple_of(i * TILE, TILE)
         c = cot_v[pl.ds(base, TILE), :]
         cot_t[:, pl.ds(base, TILE)] = c.T
-        return acc + c.astype(F32).reshape(TILE // hb, hb, hid).sum(0)
-
-    bias_part = lax.fori_loop(0, nb, cot_step, jnp.zeros((hb, hid), F32))
+        return acc + c.astype(F32).reshape(TILE // 8, 8, hid).sum(0)
+
+    bias_part = lax.fori_loop(0, nb, cot_step, jnp.zeros((8, hid), F32))
 
     def turn(part):
         drain(ft.at[:, pl.ds(part * rows, rows)], frecv.at[part])
@@ -207,81 +215,61 @@
 
         lax.fori_loop(0, count // 2, step, 0)
 
-    def reduce_nodes(g, r, k):
+    def scatter_nodes(g, r, grad, k):
+        for i in range(nn):
+            g[i] = grad[i * rp:(i + 1) * rp, :].astype(BF)
         for d in range(1, nn):
             dn = lax.rem(n + d, nn)
             remote(g.at[dn], r.at[n], ars.at[k], arr.at[k], dn, f).start()
         r[n] = g[n]
 
-    def reduce_feat(g, r, s, q, k):
+    def share_feat(g, r, q, k, extra):
         drain(r.at[pl.ds(0, nn - 1)], arr.at[k])
         drain(g.at[pl.ds(0, nn - 1)], ars.at[k])
-        tot = r[0]
+        tot = r[0].astype(F32)
         for i in range(1, nn):
-            tot = tot + r[i]
-        for t in range(4):
-            i, j = t // 2, t % 2
-            s[t, :, 0:TILE] = tot[i * hb:(i + 1) * hb, j * TILE:(j + 1) * TILE]
-            if s.shape[2] > TILE:
-                s[t, :, TILE:] = tot[rp:, :]
+            tot = tot + r[i].astype(F32)
+        q[f, 0:rp, :] = tot
+        if extra is not None:
+            q[f, rp:, :] = extra
         for d in range(1, nf):
-            df = lax.rem(f + d, nf)
-            remote(s.at[df // 2], q.at[f], ars.at[k + 1], arr.at[k + 1], n, df).start()
-        q[f] = s[f // 2]
-
-    def back_feat(s, q, c, k):
+            remote(q.at[f], q.at[f], ars.at[k + 1], arr.at[k + 1], n, lax.rem(f + d, nf)).start()
+
+    def gather_nodes(q, half, k):
         drain(q.at[pl.ds(0, nf - 1)], arr.at[k + 1])
         drain(q.at[pl.ds(0, nf - 1)], ars.at[k + 1])
         tot = q[0]
         for i in range(1, nf):
             tot = tot + q[i]
-        if q.shape[2] > TILE:
-            gb_out[...] = jnp.sum(tot[:, TILE:], axis=0, keepdims=True)
-        y = f // 2
-        c[y] = tot[:, 0:TILE]
-        for d in (2, 4, 6):
-            remote(c.at[y], c.at[y], ars.at[k + 2], arr.at[k + 2], n, lax.rem(f + d, nf)).start()
-
-    def back_nodes(c, half, k):
-        drain(c.at[pl.ds(0, 3)], arr.at[k + 2])
-        drain(c.at[pl.ds(0, 3)], ars.at[k + 2])
         at = pl.ds(pl.multiple_of(half * hid + n * rp, rp), rp)
-        gfin[at, :] = jnp.concatenate(
-            [jnp.concatenate([c[0], c[1]], axis=1), jnp.concatenate([c[2], c[3]], axis=1)], axis=0)
+        gfin[at, :] = tot[0:rp, :].astype(BF)
         for d in range(1, nn):
-            remote(gfin.at[at], gfin.at[at], ars.at[k + 3], arr.at[k + 3], lax.rem(n + d, nn), f).start()
+            remote(gfin.at[at], gfin.at[at], ars.at[k + 2], arr.at[k + 2], lax.rem(n + d, nn), f).start()
+        if half == 0:
+            bslot[n] = tot[rp:, :]
+            for d in range(1, nn):
+                remote(bslot.at[n], bslot.at[n], ars.at[6], arr.at[6], lax.rem(n + d, nn), f).start()
 
     def finish(half, k):
         some = gfin.at[pl.ds(half * hid, (nn - 1) * rp)]
-        drain(some, arr.at[k + 3])
-        drain(some, ars.at[k + 3])
+        drain(some, arr.at[k + 2])
+        drain(some, ars.at[k + 2])
         at = pl.ds(half * hid, hid)
         return pltpu.make_async_copy(gfin.at[at], gw_hbm.at[at], load_sem.at[4 + half])
-
-    forward(0)
-    hidden(nb, nb)
-    if nch > 1:
-        forward(1)
-    g_top = dot(cot_t[...], hn[nb:2 * nb].reshape(rows, hid)).T
-    for i in range(nn):
-        gt[i, 0:rp, :] = g_top[i * rp:(i + 1) * rp, :]
-        gt[i, rp:, :] = bias_part
-    reduce_nodes(gt, rt, 0)
-    for c in range(2, nch):
-        forward(c)
-    hidden(in_base, nb)
-    reduce_feat(gt, rt, st, qt, 0)
 
     def halo(c):
         drain(at_rows(out_base, c), pfwd.at[c])
         hidden(out_base + c * ch, ch)
 
-    halo(0)
-    back_feat(st, qt, ct, 0)
-    if nch > 1:
-        halo(1)
-    back_nodes(ct, 0, 0)
-    for c in range(2, nch):
+    hidden(nb, nb)
+    scatter_nodes(gt, rt, dot(cot_t[...], hn[nb:2 * nb].reshape(rows, hid)).T, 0)
+    for c in range(nch):
+        forward(c)
+        if c == min(1, nch - 1):
+            share_feat(gt, rt, qt, 0, bias_part)
+    hidden(in_base, nb)
+    gather_nodes(qt, 0, 0)
+    for c in range(nch):
         halo(c)
 
     loads[3].wait()
@@ -301,12 +289,13 @@
 
     lax.fori_loop(0, nch, two_chunk, 0)
 
-    g_bot = dot(cot_t[...], mn[...]).T
-    for i in range(nn):
-        gb[i] = g_bot[i * rp:(i + 1) * rp, :]
-    reduce_nodes(gb, rb, 4)
+    scatter_nodes(gb, rb, dot(cot_t[...], mn[...]).T, 3)
     top = finish(0, 0)
     top.start()
+    drain(bslot.at[pl.ds(0, nn - 1)], arr.at[6])
+    drain(bslot.at[pl.ds(0, nn - 1)], ars.at[6])
+    bias = pltpu.make_async_copy(bslot, gb_hbm, load_sem.at[6])
+    bias.start()
 
     for part in range(3):
         drain(ft.at[pl.ds(0, (nf - 1) * fd), pl.ds(0, rows)], fsend.at[part])
@@ -330,14 +319,14 @@
         def _():
             drain(at_rows(in_base, c), pfsend.at[c])
 
-    reduce_feat(gb, rb, sb, qb, 4)
-    back_feat(sb, qb, cb, 4)
-    back_nodes(cb, 1, 4)
+    share_feat(gb, rb, qb, 3, None)
+    gather_nodes(qb, 1, 3)
     for c in range(nch):
         drain(out_v.at[pl.ds(c * cr, cr)], out_sem.at[c])
-    bottom = finish(1, 4)
+    bottom = finish(1, 3)
     bottom.start()
     top.wait()
+    bias.wait()
     bottom.wait()
 
 
@@ -348,7 +337,6 @@
     hid = b_one.shape[0]
     features = w_one.shape[0]
     rp = hid // nn
-    hb = rp // 2
     ch = min(4, nb)
     nch = nb // ch
     anyspace = pl.BlockSpec(memory_space=pl.ANY)
@@ -359,11 +347,11 @@
         functools.partial(kernel, nn, nf, nb, neigh, ch),
         out_shape=(
             jax.ShapeDtypeStruct((rows, hid), BF),
-            jax.ShapeDtypeStruct((2 * hid, hid), F32),
-            jax.ShapeDtypeStruct((1, hid), F32),
+            jax.ShapeDtypeStruct((2 * hid, hid), BF),
+            jax.ShapeDtypeStruct((nn, 8, hid), F32),
         ),
         in_specs=[anyspace, sm, anyspace, anyspace, vm, anyspace, vm, anyspace],
-        out_specs=(anyspace, anyspace, vm),
+        out_specs=(anyspace,) * 3,
         scratch_shapes=[
             pltpu.VMEM((features, 3 * rows), BF),
             pltpu.VMEM((3 * nb, TILE, features), BF),
@@ -376,25 +364,33 @@
             pltpu.VMEM(w_one.shape, BF),
             pltpu.VMEM(w_two.shape, BF),
             pltpu.VMEM((rows, hid), BF),
-            pltpu.VMEM((nn, rp + hb, hid), F32),
-            pltpu.VMEM((nn, rp + hb, hid), F32),
-            pltpu.VMEM((4, hb, TILE + hid), F32),
-            pltpu.VMEM((nf, hb, TILE + hid), F32),
-            pltpu.VMEM((4, hb, TILE), F32),
-            pltpu.VMEM((nn, rp, hid), F32),
-            pltpu.VMEM((nn, rp, hid), F32),
-            pltpu.VMEM((4, hb, TILE), F32),
-            pltpu.VMEM((nf, hb, TILE), F32),
-            pltpu.VMEM((4, hb, TILE), F32),
-            pltpu.VMEM((2 * hid, hid), F32),
-            dma((6,)), dma((3,)), dma((3,)), dma((3,)),
+            pltpu.VMEM((nn, rp, hid), BF),
+            pltpu.VMEM((nn, rp, hid), BF),
+            pltpu.VMEM((nf, rp + 8, hid), F32),
+            pltpu.VMEM((nn, rp, hid), BF),
+            pltpu.VMEM((nn, rp, hid), BF),
+            pltpu.VMEM((nf, rp, hid), F32),
+            pltpu.VMEM((2 * hid, hid), BF),
+            pltpu.VMEM((nn, 8, hid), F32),
+            dma((7,)), dma((3,)), dma((3,)), dma((3,)),
             dma((nch,)), dma((nch,)), dma((nch,)), dma((nch,)), dma((nch,)),
-            dma((8,)), dma((8,)), dma((nch,)),
+            dma((7,)), dma((7,)), dma((nch,)),
         ],
         compiler_params=pltpu.CompilerParams(
             collective_id=0, has_side_effects=True, vmem_limit_bytes=56 * 2**20),
         name="sage",
     )(feats, tile_src, tile_weight, w_one, b_one.reshape(1, hid), w_two, b_two.reshape(1, hid), cotangent)
+    out, gw, gb = pl.pallas_call(
+        hand_over,
+        out_shape=(
+            jax.ShapeDtypeStruct((rows, hid), BF),
+            jax.ShapeDtypeStruct((2 * hid, hid), F32),
+            jax.ShapeDtypeStruct((1, hid), F32),
+        ),
+        in_specs=[vm] * 3,
+        out_specs=(vm,) * 3,
+        name="hand_over",
+    )(out, gw, gb)
     return out, gw, gb.reshape(hid)
 
 

time: 92.6 us -> 80.5 us (0.87)
  Pallas kernels: 86.3 us -> 79.7 us
  local copies, waits for them, and re-layouts: 5.36 us -> 0 us
    pallas_call x1, Pallas kernels: 86.3 us -> 77.2 us  [per_device(): pl.pallas_call(functools.partial(kernel, nn, nf, nb, neigh, ch), out_shap...]
    unnamed x3 -> x0, local copies, waits for them, and re-layouts: 5.36 us -> none
    pallas_call x0 -> x1, Pallas kernels: none -> 2.51 us  [per_device(): pl.pallas_call(hand_over, out_shape=(jax.ShapeDtypeStruct((rows, hid), BF...]
where the time goes in v3:
time: 80.5 us; the launch traced here: 80.3 us
  Pallas kernels  79.7 us (99%)
    pallas_call x1, Pallas kernels, per_device(): pl.pallas_call(functools.partial(kernel, nn, nf, nb, neigh, ch), out_shap...  77.2 us
    pallas_call x1, Pallas kernels, per_device(): pl.pallas_call(hand_over, out_shape=(jax.ShapeDtypeStruct((rows, hid), BF...  2.51 us

profile of v3, /device:TPU:1, one launch (start us, length us, event | category | flops | bytes accessed | tf_op | source)
XLA Modules:
  0.0 80.3 jit_solution(17861901914172708917)
XLA Ops:
  0.6 77.2 %sage.1 = (bf16[2048,256]{1,0:T(8,128)(2,1)}, bf16[512,256]{1,0:T(8,128)(2,1)}, f32[16,8,256]{2,1,0:T(8,128)}) custom-call(bf16[16,16384]{1,0:T(8,128)(2,1)} %feats.1, s32[16,20]{1,0:T(8,128)} %src.1, bf16[16,20,128,128]{3,2,1,0:T(8,128)(2,1)} %a_hbm.1, bf16[128,512]{1,0:T(8,128)(2,1)} %w1_hbm.1, f32[1,256]{1,0:T(1,128)} %bitcast.3, ...), custom_call_target="tpu_custom_call" | custom-call | tf_op jit(solution)/shard_map/sage/pallas_call | solution.py:346
  77.8 2.5 %hand_over.1 = (bf16[2048,256]{1,0:T(8,128)(2,1)}, f32[512,256]{1,0:T(8,128)}, f32[1,256]{1,0:T(1,128)}) custom-call(bf16[2048,256]{1,0:T(8,128)(2,1)} %get-tuple-element.9.out, bf16[512,256]{1,0:T(8,128)(2,1)} %get-tuple-element.10.gw, f32[16,8,256]{2,1,0:T(8,128)} %get-tuple-element.11.gb), custom_call_target="tpu_custom_call" | custom-call | tf_op jit(solution)/shard_map/hand_over/pallas_call | solution.py:383

commit v4 on v3

--- a/solution.py
+++ b/solution.py
@@ -25,6 +25,10 @@
 
 def dot(a, b):
     return lax.dot_general(a, b, (((1,), (0,)), ((), ())), preferred_element_type=F32)
+
+
+def dot_nt(a, b):
+    return lax.dot_general(a, b, (((1,), (1,)), ((), ())), preferred_element_type=F32)
 
 
 def hand_over(out, gw, gb, out_copy, gw_wide, gb_sum):
@@ -39,9 +43,9 @@
 def kernel(nn, nf, nb, neigh, chunk_blocks,
            feats, src, a_hbm, w1_hbm, b1, w2_hbm, b2, cot_hbm,
            out_hbm, gw_hbm, gb_hbm,
-           ft, fn, a_v, pn, hn, mn, cot_v, cot_t, w1_v, w2_v, out_v,
+           ft, zb, fa, fb, a_v, pt, hn, mn, cot_v, cot_t, w1_v, w2_v, out_v,
            gt, rt, qt, gb, rb, qb, gfin, bslot,
-           load_sem, fsend, fedge, frecv, psend, pbound, pfsend, pdir, pfwd,
+           load_sem, zsend, zrecv, fsend, fedge, frecv, psend, pbound, pfsend, pdir, pfwd,
            ars, arr, out_sem):
     fd = feats.shape[0]
     rows = nb * TILE
@@ -87,36 +91,65 @@
 
     pl.semaphore_wait(barrier, nf + nn)
 
-    def feat_copy(part, d):
-        df = lax.rem(f + d, nf)
-        j = lax.rem(df + nf + part - 1, nf)
-        if part == 0:
-            dn = jnp.where(df == 0, n_next, n)
-        elif part == 2:
-            dn = jnp.where(df == nf - 1, n_prev, n)
+    partner = f + 1 - 2 * z
+    half = nf * fd // 2
+    row_own = (f // 2) * fd + z * half
+    row_other = (f // 2) * fd + (1 - z) * half
+
+    def columns(j):
+        return pl.ds(pl.multiple_of(j * rows, rows), rows)
+
+    for t in range(nf):
+        j = lax.rem(partner + t, nf)
+        remote(feats.at[:, columns(j)], zb.at[:, columns(j)], zsend.at[0], zrecv.at[t], n, partner).start()
+
+    def spread(t, source, row, h):
+        j = lax.rem(f + t, nf)
+        s = source.at[:, columns(j)]
+
+        def to(part):
+            return ft.at[pl.ds(pl.multiple_of(row, fd), fd), pl.ds(part * rows, rows)]
+
+        def keep(part):
+            pltpu.make_async_copy(s, to(part), frecv.at[h]).start()
+
+        if t % 2 == 0:
+            if t == 0:
+                keep(1)
+            else:
+                remote(s, to(1), fsend.at[h], frecv.at[h], n, j).start()
+            return
+        dn = jnp.where(j == nf - 1, n_next, n)
+        df = lax.rem(j + 1, nf)
+        if t == nf - 1:
+            @pl.when(f == 0)
+            def _():
+                remote(s, to(0), fedge.at[h], frecv.at[h], dn, df).start()
+
+            @pl.when(f != 0)
+            def _():
+                keep(0)
         else:
-            dn = n
-        s = feats.at[:, pl.ds(pl.multiple_of(j * rows, rows), rows)]
-        t = ft.at[pl.ds(pl.multiple_of(f * fd, fd), fd), pl.ds(part * rows, rows)]
-        return s, t, dn, df
-
-    for part in (1, 0, 2):
-        for d in range(1, nf):
-            s, t, dn, df = feat_copy(part, d)
-            remote(s, t, fsend.at[part], frecv.at[part], dn, df).start()
-        s, t, dn, df = feat_copy(part, 0)
-        if part == 1:
-            pltpu.make_async_copy(s, t, frecv.at[part]).start()
+            remote(s, to(0), fsend.at[h], frecv.at[h], dn, df).start()
+        dn = jnp.where(j == 0, n_prev, n)
+        df = lax.rem(j + nf - 1, nf)
+        if t == 1:
+            @pl.when(f == nf - 1)
+            def _():
+                remote(s, to(2), fedge.at[h], frecv.at[h], dn, df).start()
+
+            @pl.when(f != nf - 1)
+            def _():
+                keep(2)
         else:
-            edge = f == (0 if part == 0 else nf - 1)
-
-            @pl.when(edge)
-            def _():
-                remote(s, t, fedge.at[part], frecv.at[part], dn, df).start()
-
-            @pl.when(jnp.logical_not(edge))
-            def _():
-                pltpu.make_async_copy(s, t, frecv.at[part]).start()
+            remote(s, to(2), fsend.at[h], frecv.at[h], dn, df).start()
+
+    for t in range(nf):
+        spread(t, feats, row_own, 0)
+
+    def pass_on(t):
+        drain(zb.at[:, pl.ds(0, rows)], zrecv.at[t])
+        spread(t, zb, row_other, 1)
 
     loads[1].wait()
 
@@ -126,90 +159,107 @@
         cot_t[:, pl.ds(base, TILE)] = c.T
         return acc + c.astype(F32).reshape(TILE // 8, 8, hid).sum(0)
 
-    bias_part = lax.fori_loop(0, nb, cot_step, jnp.zeros((8, hid), F32))
-
-    def turn(part):
-        drain(ft.at[:, pl.ds(part * rows, rows)], frecv.at[part])
-
-        def step(i, carry):
-            base = pl.multiple_of(part * rows + i * TILE, TILE)
-            fn[part * nb + i] = ft[:, pl.ds(base, TILE)].T
-            return carry
-
-        lax.fori_loop(0, nb, step, 0, unroll=2)
-
-    turn(1)
-    turn(0)
-    turn(2)
-    loads[0].wait()
-    loads[2].wait()
+    bias_part = lax.fori_loop(0, nb // 2, cot_step, jnp.zeros((8, hid), F32))
+    pass_on(0)
+    bias_part = lax.fori_loop(nb // 2, nb, cot_step, bias_part)
+    for t in range(1, nf - 2):
+        pass_on(t)
 
     first = (n * nf + f - 1) * nb
     total = nn * nf * nb
 
-    def gather(table, b):
-        acc = None
-        for k in range(0, neigh, 2):
-            picked = []
-            for i in (k, k + 1):
-                s = src[b, i] - first
-                s = jnp.where(s >= total, s - total, s)
-                s = jnp.where(s < 0, s + total, s)
-                s = jnp.minimum(s, 3 * nb - 1)
-                picked.append(table[s])
-            p = dot(jnp.concatenate([a_v[b, k], a_v[b, k + 1]], axis=1),
-                    jnp.concatenate(picked, axis=0))
-            acc = p if acc is None else acc + p
-        return acc
-
-    partner = f + 1 - 2 * z
+    def pick(table, b, k):
+        s = src[b, k] - first
+        s = jnp.where(s >= total, s - total, s)
+        s = jnp.where(s < 0, s + total, s)
+        return table[jnp.minimum(s, 3 * nb - 1)]
+
+    def pair(b, k):
+        return jnp.concatenate([a_v[b, k], a_v[b, k + 1]], axis=1)
+
     bound_next = jnp.logical_and(f == nf - 1, lax.rem(n, 2) == 1)
     bound_prev = jnp.logical_and(f == 0, lax.rem(n, 2) == 0)
     out_base = z * (2 * nb)
     in_base = (2 - 2 * z) * nb
 
-    def at_rows(base, c):
-        return pn.at[pl.ds(base + c * ch, ch)]
-
-    def one_chunk(c, carry):
+    def at_cols(row, base, c):
+        return pt.at[pl.ds(pl.multiple_of(row, half), half),
+                     pl.ds(pl.multiple_of((base + c * ch) * TILE, cr), cr)]
+
+    def arrange(table, row, h):
+        drain(ft.at[pl.ds(0, half)], frecv.at[h])
+
+        def step(i, carry):
+            table[i] = ft[pl.ds(pl.multiple_of(row, half), half), pl.ds(pl.multiple_of(i * TILE, TILE), TILE)]
+            return carry
+
+        lax.fori_loop(0, 3 * nb, step, 0, unroll=4)
+
+    def one_chunk(table, row, h, c):
         for i in range(ch):
             b = c * ch + i
-            pn[nb + b] = gather(fn, b).astype(BF)
-        own = at_rows(nb, c)
-        remote(own, at_rows(out_base, c), psend.at[c], pdir.at[c], n, partner).start()
+            acc = None
+            for k in range(0, neigh, 2):
+                p = dot_nt(jnp.concatenate([pick(table, b, k), pick(table, b, k + 1)], axis=1), pair(b, k))
+                acc = p if acc is None else acc + p
+            pt[pl.ds(pl.multiple_of(row, half), half),
+               pl.ds(pl.multiple_of((nb + b) * TILE, TILE), TILE)] = acc.astype(BF)
+        m = h * nch + c
+        own = at_cols(row, nb, c)
+        remote(own, at_cols(row, out_base, c), psend.at[m], pdir.at[m], n, partner).start()
 
         @pl.when(bound_next)
         def _():
-            remote(own, at_rows(0, c), pbound.at[c], pfwd.at[c], n_next, jnp.int32(0)).start()
+            remote(own, at_cols(row, 0, c), pbound.at[m], pfwd.at[m], n_next, jnp.int32(0)).start()
 
         @pl.when(bound_prev)
         def _():
-            remote(own, at_rows(2 * nb, c), pbound.at[c], pfwd.at[c], n_prev, jnp.int32(nf - 1)).start()
-
-        return carry
-
-    lax.fori_loop(0, nch, one_chunk, 0)
+            remote(own, at_cols(row, 2 * nb, c), pbound.at[m], pfwd.at[m], n_prev, jnp.int32(nf - 1)).start()
 
     skip = jnp.logical_or(jnp.logical_and(f == nf - 2, lax.rem(n, 2) == 1),
                           jnp.logical_and(f == 1, lax.rem(n, 2) == 0))
     fwd_f = lax.rem(f + jnp.where(z == 0, 2, nf - 2), nf)
     fwd_n = jnp.where(f == nf - 2, n_next, jnp.where(f == 1, n_prev, n))
 
-    def forward(c):
-        drain(at_rows(in_base, c), pdir.at[c])
+    def forward(h, c):
+        m = h * nch + c
+        row = (1 - z) * half if h == 0 else z * half
+        came = at_cols(row, in_base, c)
+        drain(came, pdir.at[m])
 
         @pl.when(jnp.logical_not(skip))
         def _():
-            remote(at_rows(in_base, c), at_rows(out_base, c), pfsend.at[c], pfwd.at[c], fwd_n, fwd_f).start()
-
-    w_cat = jnp.concatenate([w1_v[:, :hid], w1_v[:, hid:]], axis=0)
+            remote(came, at_cols(row, out_base, c), pfsend.at[m], pfwd.at[m], fwd_n, fwd_f).start()
+
+    arrange(fa, z * half, 0)
+    loads[2].wait()
+    one_chunk(fa, z * half, 0, 0)
+    pass_on(nf - 2)
+    if nch > 1:
+        one_chunk(fa, z * half, 0, 1)
+    pass_on(nf - 1)
+    if nch > 2:
+        lax.fori_loop(2, nch, lambda c, u: (one_chunk(fa, z * half, 0, c), u)[1], 0)
+    arrange(fb, (1 - z) * half, 1)
+
+    def second(c, carry):
+        one_chunk(fb, (1 - z) * half, 1, c)
+        forward(0, c)
+        return carry
+
+    lax.fori_loop(0, nch, second, 0)
+
+    loads[0].wait()
+    order = [g * fd for g in range(0, nf, 2)] + [g * fd for g in range(1, nf, 2)]
+    w_cat = jnp.concatenate(
+        [w1_v[g:g + fd, :hid] for g in order] + [w1_v[g:g + fd, hid:] for g in order], axis=0)
     bias_one = b1[...]
 
     def hidden(base, count):
         def step(i, carry):
             at = pl.ds(base + i * 2, 2)
-            fp = jnp.concatenate([fn[at], pn[at]], axis=2).reshape(2 * TILE, 2 * TILE)
-            v = dot(fp, w_cat) + bias_one
+            cols = pl.ds(pl.multiple_of((base + i * 2) * TILE, 2 * TILE), 2 * TILE)
+            v = dot(jnp.concatenate([ft[:, cols], pt[:, cols]], axis=0).T, w_cat) + bias_one
             hn[at] = jnp.maximum(v, 0.0).astype(BF).reshape(2, TILE, hid)
             return carry
 
@@ -258,13 +308,14 @@
         return pltpu.make_async_copy(gfin.at[at], gw_hbm.at[at], load_sem.at[4 + half])
 
     def halo(c):
-        drain(at_rows(out_base, c), pfwd.at[c])
+        for h in range(2):
+            drain(at_cols(0, out_base, c), pfwd.at[h * nch + c])
         hidden(out_base + c * ch, ch)
 
     hidden(nb, nb)
     scatter_nodes(gt, rt, dot(cot_t[...], hn[nb:2 * nb].reshape(rows, hid)).T, 0)
     for c in range(nch):
-        forward(c)
+        forward(1, c)
         if c == min(1, nch - 1):
             share_feat(gt, rt, qt, 0, bias_part)
     hidden(in_base, nb)
@@ -279,7 +330,11 @@
         for i in range(ch):
             b = c * ch + i
             at = pl.ds(pl.multiple_of(b * TILE, TILE), TILE)
-            mn[at, :] = gather(hn, b).astype(BF)
+            acc = None
+            for k in range(0, neigh, 2):
+                p = dot(pair(b, k), jnp.concatenate([pick(hn, b, k), pick(hn, b, k + 1)], axis=0))
+                acc = p if acc is None else acc + p
+            mn[at, :] = acc.astype(BF)
         at = pl.ds(pl.multiple_of(c * cr, cr), cr)
         own = hn[pl.ds(nb + c * ch, ch)].reshape(cr, hid)
         both = jnp.concatenate([own, mn[at, :]], axis=1)
@@ -297,27 +352,25 @@
     bias = pltpu.make_async_copy(bslot, gb_hbm, load_sem.at[6])
     bias.start()
 
-    for part in range(3):
-        drain(ft.at[pl.ds(0, (nf - 1) * fd), pl.ds(0, rows)], fsend.at[part])
-
-    @pl.when(f == 0)
-    def _():
-        drain(ft.at[pl.ds(0, fd), pl.ds(0, rows)], fedge.at[0])
-
-    @pl.when(f == nf - 1)
-    def _():
-        drain(ft.at[pl.ds(0, fd), pl.ds(0, rows)], fedge.at[2])
-
-    for c in range(nch):
-        drain(at_rows(nb, c), psend.at[c])
+    drain(zb, zsend.at[0])
+    for h in range(2):
+        drain(ft.at[pl.ds(0, (nf + 1) * fd // 3), :], fsend.at[h])
+
+        @pl.when(jnp.logical_or(f == 0, f == nf - 1))
+        def _():
+            drain(ft.at[pl.ds(0, fd), pl.ds(0, rows)], fedge.at[h])
+
+    for m in range(2 * nch):
+        some = at_cols(0, 0, 0)
+        drain(some, psend.at[m])
 
         @pl.when(jnp.logical_or(bound_next, bound_prev))
         def _():
-            drain(at_rows(nb, c), pbound.at[c])
+            drain(some, pbound.at[m])
 
         @pl.when(jnp.logical_not(skip))
         def _():
-            drain(at_rows(in_base, c), pfsend.at[c])
+            drain(some, pfsend.at[m])
 
     share_feat(gb, rb, qb, 3, None)
     gather_nodes(qb, 1, 3)
@@ -354,9 +407,11 @@
         out_specs=(anyspace,) * 3,
         scratch_shapes=[
             pltpu.VMEM((features, 3 * rows), BF),
-            pltpu.VMEM((3 * nb, TILE, features), BF),
+            pltpu.VMEM((fd, nf * rows), BF),
+            pltpu.VMEM((3 * nb, features // 2, TILE), BF),
+            pltpu.VMEM((3 * nb, features // 2, TILE), BF),
             pltpu.VMEM(tile_weight.shape, BF),
-            pltpu.VMEM((3 * nb, TILE, features), BF),
+            pltpu.VMEM((features, 3 * rows), BF),
             pltpu.VMEM((3 * nb, TILE, hid), BF),
             pltpu.VMEM((rows, hid), BF),
             pltpu.VMEM((rows, hid), BF),
@@ -372,8 +427,8 @@
             pltpu.VMEM((nf, rp, hid), F32),
             pltpu.VMEM((2 * hid, hid), BF),
             pltpu.VMEM((nn, 8, hid), F32),
-            dma((7,)), dma((3,)), dma((3,)), dma((3,)),
-            dma((nch,)), dma((nch,)), dma((nch,)), dma((nch,)), dma((nch,)),
+            dma((7,)), dma((1,)), dma((nf,)), dma((2,)), dma((2,)), dma((2,)),
+            dma((2 * nch,)), dma((2 * nch,)), dma((2 * nch,)), dma((2 * nch,)), dma((2 * nch,)),
             dma((7,)), dma((7,)), dma((nch,)),
         ],
         compiler_params=pltpu.CompilerParams(

time: 80.5 us -> 77.8 us (0.966)
  Pallas kernels: 79.7 us -> 77 us
    pallas_call x1, Pallas kernels: 77.2 us -> 74.5 us  [per_device(): pl.pallas_call(functools.partial(kernel, nn, nf, nb, neigh, ch), out_shap...]
where the time goes in v4:
time: 77.8 us; the launch traced here: 77.7 us
  Pallas kernels  77 us (99%)
    pallas_call x1, Pallas kernels, per_device(): pl.pallas_call(functools.partial(kernel, nn, nf, nb, neigh, ch), out_shap...  74.5 us
    pallas_call x1, Pallas kernels, per_device(): pl.pallas_call(hand_over, out_shape=(jax.ShapeDtypeStruct((rows, hid), BF...  2.51 us

profile of v4, /device:TPU:1, one launch (start us, length us, event | category | flops | bytes accessed | tf_op | source)
XLA Modules:
  0.0 77.7 jit_solution(8334531575620067209)
XLA Ops:
  0.6 74.5 %sage.1 = (bf16[2048,256]{1,0:T(8,128)(2,1)}, bf16[512,256]{1,0:T(8,128)(2,1)}, f32[16,8,256]{2,1,0:T(8,128)}) custom-call(bf16[16,16384]{1,0:T(8,128)(2,1)} %feats.1, s32[16,20]{1,0:T(8,128)} %src.1, bf16[16,20,128,128]{3,2,1,0:T(8,128)(2,1)} %a_hbm.1, bf16[128,512]{1,0:T(8,128)(2,1)} %w1_hbm.1, f32[1,256]{1,0:T(1,128)} %bitcast.3, ...), custom_call_target="tpu_custom_call" | custom-call | tf_op jit(solution)/shard_map/sage/pallas_call | solution.py:399
  75.1 2.5 %hand_over.1 = (bf16[2048,256]{1,0:T(8,128)(2,1)}, f32[512,256]{1,0:T(8,128)}, f32[1,256]{1,0:T(1,128)}) custom-call(bf16[2048,256]{1,0:T(8,128)(2,1)} %get-tuple-element.9.out, bf16[512,256]{1,0:T(8,128)(2,1)} %get-tuple-element.10.gw, f32[16,8,256]{2,1,0:T(8,128)} %get-tuple-element.11.gb), custom_call_target="tpu_custom_call" | custom-call | tf_op jit(solution)/shard_map/hand_over/pallas_call | solution.py:438

commit v5 on v4

--- a/solution.py
+++ b/solution.py
@@ -99,7 +99,8 @@
     def columns(j):
         return pl.ds(pl.multiple_of(j * rows, rows), rows)
 
-    for t in range(nf):
+    far_first = sorted(range(nf), key=lambda t: (abs(t - nf // 2), t))
+    for t in far_first:
         j = lax.rem(partner + t, nf)
         remote(feats.at[:, columns(j)], zb.at[:, columns(j)], zsend.at[0], zrecv.at[t], n, partner).start()
 
@@ -144,7 +145,7 @@
         else:
             remote(s, to(2), fsend.at[h], frecv.at[h], dn, df).start()
 
-    for t in range(nf):
+    for t in far_first:
         spread(t, feats, row_own, 0)
 
     def pass_on(t):
@@ -160,9 +161,9 @@
         return acc + c.astype(F32).reshape(TILE // 8, 8, hid).sum(0)
 
     bias_part = lax.fori_loop(0, nb // 2, cot_step, jnp.zeros((8, hid), F32))
-    pass_on(0)
+    pass_on(far_first[0])
     bias_part = lax.fori_loop(nb // 2, nb, cot_step, bias_part)
-    for t in range(1, nf - 2):
+    for t in far_first[1:-2]:
         pass_on(t)
 
     first = (n * nf + f - 1) * nb
@@ -234,17 +235,19 @@
     arrange(fa, z * half, 0)
     loads[2].wait()
     one_chunk(fa, z * half, 0, 0)
-    pass_on(nf - 2)
+    pass_on(far_first[-2])
     if nch > 1:
         one_chunk(fa, z * half, 0, 1)
-    pass_on(nf - 1)
+    pass_on(far_first[-1])
     if nch > 2:
         lax.fori_loop(2, nch, lambda c, u: (one_chunk(fa, z * half, 0, c), u)[1], 0)
     arrange(fb, (1 - z) * half, 1)
 
+    for c in range(nch):
+        forward(0, c)
+
     def second(c, carry):
         one_chunk(fb, (1 - z) * half, 1, c)
-        forward(0, c)
         return carry
 
     lax.fori_loop(0, nch, second, 0)
@@ -275,7 +278,6 @@
 
     def share_feat(g, r, q, k, extra):
         drain(r.at[pl.ds(0, nn - 1)], arr.at[k])
-        drain(g.at[pl.ds(0, nn - 1)], ars.at[k])
         tot = r[0].astype(F32)
         for i in range(1, nn):
             tot = tot + r[i].astype(F32)
@@ -287,7 +289,6 @@
 
     def gather_nodes(q, half, k):
         drain(q.at[pl.ds(0, nf - 1)], arr.at[k + 1])
-        drain(q.at[pl.ds(0, nf - 1)], ars.at[k + 1])
         tot = q[0]
         for i in range(1, nf):
             tot = tot + q[i]
@@ -303,7 +304,6 @@
     def finish(half, k):
         some = gfin.at[pl.ds(half * hid, (nn - 1) * rp)]
         drain(some, arr.at[k + 2])
-        drain(some, ars.at[k + 2])
         at = pl.ds(half * hid, hid)
         return pltpu.make_async_copy(gfin.at[at], gw_hbm.at[at], load_sem.at[4 + half])
 
@@ -313,18 +313,16 @@
         hidden(out_base + c * ch, ch)
 
     hidden(nb, nb)
+    for c in range(min(2, nch)):
+        forward(1, c)
     scatter_nodes(gt, rt, dot(cot_t[...], hn[nb:2 * nb].reshape(rows, hid)).T, 0)
-    for c in range(nch):
+    for c in range(2, nch):
         forward(1, c)
-        if c == min(1, nch - 1):
-            share_feat(gt, rt, qt, 0, bias_part)
     hidden(in_base, nb)
-    gather_nodes(qt, 0, 0)
-    for c in range(nch):
+    for c in range(nch - 1):
         halo(c)
-
-    loads[3].wait()
-    bias_two = b2[...]
+    share_feat(gt, rt, qt, 0, bias_part)
+    halo(nch - 1)
 
     def two_chunk(c, carry):
         for i in range(ch):
@@ -335,6 +333,15 @@
                 p = dot(pair(b, k), jnp.concatenate([pick(hn, b, k), pick(hn, b, k + 1)], axis=0))
                 acc = p if acc is None else acc + p
             mn[at, :] = acc.astype(BF)
+        return carry
+
+    lax.fori_loop(0, nch, two_chunk, 0)
+    scatter_nodes(gb, rb, dot(cot_t[...], mn[...]).T, 3)
+
+    loads[3].wait()
+    bias_two = b2[...]
+
+    def out_chunk(c, carry):
         at = pl.ds(pl.multiple_of(c * cr, cr), cr)
         own = hn[pl.ds(nb + c * ch, ch)].reshape(cr, hid)
         both = jnp.concatenate([own, mn[at, :]], axis=1)
@@ -342,38 +349,42 @@
         pltpu.make_async_copy(out_v.at[at], out_hbm.at[at], out_sem.at[c]).start()
         return carry
 
-    lax.fori_loop(0, nch, two_chunk, 0)
-
-    scatter_nodes(gb, rb, dot(cot_t[...], mn[...]).T, 3)
+    lax.fori_loop(0, nch, out_chunk, 0)
+    gather_nodes(qt, 0, 0)
+
+    share_feat(gb, rb, qb, 3, None)
+
+    drain(zb, zsend.at[0])
+    for h in range(2):
+        drain(ft.at[pl.ds(0, (nf + 1) * fd // 3), :], fsend.at[h])
+
+        @pl.when(jnp.logical_or(f == 0, f == nf - 1))
+        def _():
+            drain(ft.at[pl.ds(0, fd), pl.ds(0, rows)], fedge.at[h])
+
+    for m in range(2 * nch):
+        some = at_cols(0, 0, 0)
+        drain(some, psend.at[m])
+
+        @pl.when(jnp.logical_or(bound_next, bound_prev))
+        def _():
+            drain(some, pbound.at[m])
+
+        @pl.when(jnp.logical_not(skip))
+        def _():
+            drain(some, pfsend.at[m])
+
+    gather_nodes(qb, 1, 3)
     top = finish(0, 0)
     top.start()
     drain(bslot.at[pl.ds(0, nn - 1)], arr.at[6])
-    drain(bslot.at[pl.ds(0, nn - 1)], ars.at[6])
     bias = pltpu.make_async_copy(bslot, gb_hbm, load_sem.at[6])
     bias.start()
-
-    drain(zb, zsend.at[0])
-    for h in range(2):
-        drain(ft.at[pl.ds(0, (nf + 1) * fd // 3), :], fsend.at[h])
-
-        @pl.when(jnp.logical_or(f == 0, f == nf - 1))
-        def _():
-            drain(ft.at[pl.ds(0, fd), pl.ds(0, rows)], fedge.at[h])
-
-    for m in range(2 * nch):
-        some = at_cols(0, 0, 0)
-        drain(some, psend.at[m])
-
-        @pl.when(jnp.logical_or(bound_next, bound_prev))
-        def _():
-            drain(some, pbound.at[m])
-
-        @pl.when(jnp.logical_not(skip))
-        def _():
-            drain(some, pfsend.at[m])
-
-    share_feat(gb, rb, qb, 3, None)
-    gather_nodes(qb, 1, 3)
+    for k, (g, q) in ((0, (gt, qt)), (3, (gb, qb))):
+        drain(g.at[pl.ds(0, nn - 1)], ars.at[k])
+        drain(q.at[pl.ds(0, nf - 1)], ars.at[k + 1])
+        drain(gfin.at[pl.ds(0, (nn - 1) * rp)], ars.at[k + 2])
+    drain(bslot.at[pl.ds(0, nn - 1)], ars.at[6])
     for c in range(nch):
         drain(out_v.at[pl.ds(c * cr, cr)], out_sem.at[c])
     bottom = finish(1, 3)

time: 77.8 us -> 72.7 us (0.934)
  Pallas kernels: 77 us -> 71.9 us
    pallas_call x1, Pallas kernels: 74.5 us -> 69.4 us  [per_device(): pl.pallas_call(functools.partial(kernel, nn, nf, nb, neigh, ch), out_shap...]
where the time goes in v5:
time: 72.7 us; the launch traced here: 72.5 us
  Pallas kernels  71.9 us (99%)
    pallas_call x1, Pallas kernels, per_device(): pl.pallas_call(functools.partial(kernel, nn, nf, nb, neigh, ch), out_shap...  69.4 us
    pallas_call x1, Pallas kernels, per_device(): pl.pallas_call(hand_over, out_shape=(jax.ShapeDtypeStruct((rows, hid), BF...  2.51 us

profile of v5, /device:TPU:1, one launch (start us, length us, event | category | flops | bytes accessed | tf_op | source)
XLA Modules:
  0.0 72.5 jit_solution(14767644969471196460)
XLA Ops:
  0.6 69.4 %sage.1 = (bf16[2048,256]{1,0:T(8,128)(2,1)}, bf16[512,256]{1,0:T(8,128)(2,1)}, f32[16,8,256]{2,1,0:T(8,128)}) custom-call(bf16[16,16384]{1,0:T(8,128)(2,1)} %feats.1, s32[16,20]{1,0:T(8,128)} %src.1, bf16[16,20,128,128]{3,2,1,0:T(8,128)(2,1)} %a_hbm.1, bf16[128,512]{1,0:T(8,128)(2,1)} %w1_hbm.1, f32[1,256]{1,0:T(1,128)} %bitcast.3, ...), custom_call_target="tpu_custom_call" | custom-call | tf_op jit(solution)/shard_map/sage/pallas_call | solution.py:410
  70.0 2.5 %hand_over.1 = (bf16[2048,256]{1,0:T(8,128)(2,1)}, f32[512,256]{1,0:T(8,128)}, f32[1,256]{1,0:T(1,128)}) custom-call(bf16[2048,256]{1,0:T(8,128)(2,1)} %get-tuple-element.9.out, bf16[512,256]{1,0:T(8,128)(2,1)} %get-tuple-element.10.gw, f32[16,8,256]{2,1,0:T(8,128)} %get-tuple-element.11.gb), custom_call_target="tpu_custom_call" | custom-call | tf_op jit(solution)/shard_map/hand_over/pallas_call | solution.py:449

commit v6 on v5

--- a/solution.py
+++ b/solution.py
@@ -44,7 +44,7 @@
            feats, src, a_hbm, w1_hbm, b1, w2_hbm, b2, cot_hbm,
            out_hbm, gw_hbm, gb_hbm,
            ft, zb, fa, fb, a_v, pt, hn, mn, cot_v, cot_t, w1_v, w2_v, out_v,
-           gt, rt, qt, gb, rb, qb, gfin, bslot,
+           gt, rt, qt, gb, rb, qb, gfin, bslot, g_acc,
            load_sem, zsend, zrecv, fsend, fedge, frecv, psend, pbound, pfsend, pdir, pfwd,
            ars, arr, out_sem):
     fd = feats.shape[0]
@@ -54,6 +54,9 @@
     ch = chunk_blocks
     nch = nb // ch
     cr = ch * TILE
+    plan = ([(c * ch, ch) for c in range(nch)],
+            [(c * ch, ch) for c in range(nch - 1)] + [(nb - ch, ch // 2), (nb - ch // 2, ch // 2)])
+    last = nch
     n = lax.axis_index("nodes")
     f = lax.axis_index("feat")
     z = lax.rem(f, 2)
@@ -183,9 +186,9 @@
     out_base = z * (2 * nb)
     in_base = (2 - 2 * z) * nb
 
-    def at_cols(row, base, c):
+    def at_cols(row, block, count):
         return pt.at[pl.ds(pl.multiple_of(row, half), half),
-                     pl.ds(pl.multiple_of((base + c * ch) * TILE, cr), cr)]
+                     pl.ds(pl.multiple_of(block * TILE, count * TILE), count * TILE)]
 
     def arrange(table, row, h):
         drain(ft.at[pl.ds(0, half)], frecv.at[h])
@@ -196,26 +199,32 @@
 
         lax.fori_loop(0, 3 * nb, step, 0, unroll=4)
 
-    def one_chunk(table, row, h, c):
-        for i in range(ch):
-            b = c * ch + i
+    direct_f = lax.rem(f + jnp.where(z == 0, nf - 1, 1), nf)
+    direct_n = jnp.where(f == 0, n_prev, jnp.where(f == nf - 1, n_next, n))
+    direct_base = (2 - 2 * z) * nb
+
+    def one_chunk(table, row, h, m, block, count):
+        for i in range(count):
+            b = block + i
             acc = None
             for k in range(0, neigh, 2):
                 p = dot_nt(jnp.concatenate([pick(table, b, k), pick(table, b, k + 1)], axis=1), pair(b, k))
                 acc = p if acc is None else acc + p
             pt[pl.ds(pl.multiple_of(row, half), half),
                pl.ds(pl.multiple_of((nb + b) * TILE, TILE), TILE)] = acc.astype(BF)
-        m = h * nch + c
-        own = at_cols(row, nb, c)
-        remote(own, at_cols(row, out_base, c), psend.at[m], pdir.at[m], n, partner).start()
-
-        @pl.when(bound_next)
-        def _():
-            remote(own, at_cols(row, 0, c), pbound.at[m], pfwd.at[m], n_next, jnp.int32(0)).start()
-
-        @pl.when(bound_prev)
-        def _():
-            remote(own, at_cols(row, 2 * nb, c), pbound.at[m], pfwd.at[m], n_prev, jnp.int32(nf - 1)).start()
+        own = at_cols(row, nb + block, count)
+        remote(own, at_cols(row, out_base + block, count), psend.at[m], pdir.at[m], n, partner).start()
+
+        def direct():
+            remote(own, at_cols(row, direct_base + block, count), pbound.at[m], pfwd.at[m],
+                   direct_n, direct_f).start()
+
+        if h == 1 and count < ch:
+            if block == nb - count:
+                direct()
+                return
+
+        pl.when(jnp.logical_or(bound_next, bound_prev))(direct)
 
     skip = jnp.logical_or(jnp.logical_and(f == nf - 2, lax.rem(n, 2) == 1),
                           jnp.logical_and(f == 1, lax.rem(n, 2) == 0))
@@ -224,33 +233,34 @@
 
     def forward(h, c):
         m = h * nch + c
+        block, count = plan[h][c]
         row = (1 - z) * half if h == 0 else z * half
-        came = at_cols(row, in_base, c)
+        came = at_cols(row, in_base + block, count)
         drain(came, pdir.at[m])
+        if h == 1 and c == last:
+            return
 
         @pl.when(jnp.logical_not(skip))
         def _():
-            remote(came, at_cols(row, out_base, c), pfsend.at[m], pfwd.at[m], fwd_n, fwd_f).start()
+            remote(came, at_cols(row, out_base + block, count), pfsend.at[m], pfwd.at[m], fwd_n, fwd_f).start()
 
     arrange(fa, z * half, 0)
     loads[2].wait()
-    one_chunk(fa, z * half, 0, 0)
+    one_chunk(fa, z * half, 0, 0, 0, ch)
     pass_on(far_first[-2])
     if nch > 1:
-        one_chunk(fa, z * half, 0, 1)
+        one_chunk(fa, z * half, 0, 1, ch, ch)
     pass_on(far_first[-1])
     if nch > 2:
-        lax.fori_loop(2, nch, lambda c, u: (one_chunk(fa, z * half, 0, c), u)[1], 0)
+        lax.fori_loop(2, nch, lambda c, u: (one_chunk(fa, z * half, 0, c, c * ch, ch), u)[1], 0)
     arrange(fb, (1 - z) * half, 1)
-
     for c in range(nch):
         forward(0, c)
 
-    def second(c, carry):
-        one_chunk(fb, (1 - z) * half, 1, c)
-        return carry
-
-    lax.fori_loop(0, nch, second, 0)
+    if nch > 1:
+        lax.fori_loop(0, nch - 1, lambda c, u: (one_chunk(fb, (1 - z) * half, 1, nch + c, c * ch, ch), u)[1], 0)
+    for c in (nch - 1, nch):
+        one_chunk(fb, (1 - z) * half, 1, nch + c, *plan[1][c])
 
     loads[0].wait()
     order = [g * fd for g in range(0, nf, 2)] + [g * fd for g in range(1, nf, 2)]
@@ -308,23 +318,27 @@
         return pltpu.make_async_copy(gfin.at[at], gw_hbm.at[at], load_sem.at[4 + half])
 
     def halo(c):
-        for h in range(2):
-            drain(at_cols(0, out_base, c), pfwd.at[h * nch + c])
-        hidden(out_base + c * ch, ch)
+        block, count = plan[1][c]
+        if c < nch:
+            drain(at_cols(0, *plan[0][c]), pfwd.at[c])
+        drain(at_cols(0, block, count), pfwd.at[nch + c])
+        hidden(out_base + block, count)
 
     hidden(nb, nb)
     for c in range(min(2, nch)):
         forward(1, c)
     scatter_nodes(gt, rt, dot(cot_t[...], hn[nb:2 * nb].reshape(rows, hid)).T, 0)
-    for c in range(2, nch):
+    for c in range(2, nch + 1):
         forward(1, c)
     hidden(in_base, nb)
     for c in range(nch - 1):
         halo(c)
     share_feat(gt, rt, qt, 0, bias_part)
     halo(nch - 1)
+    halo(nch)
 
     def two_chunk(c, carry):
+        turned = []
         for i in range(ch):
             b = c * ch + i
             at = pl.ds(pl.multiple_of(b * TILE, TILE), TILE)
@@ -332,11 +346,16 @@
             for k in range(0, neigh, 2):
                 p = dot(pair(b, k), jnp.concatenate([pick(hn, b, k), pick(hn, b, k + 1)], axis=0))
                 acc = p if acc is None else acc + p
-            mn[at, :] = acc.astype(BF)
+            mixed = acc.astype(BF)
+            mn[at, :] = mixed
+            turned.append(mixed.T)
+        at = pl.ds(pl.multiple_of(c * cr, cr), cr)
+        g_acc[...] += dot(jnp.concatenate(turned, axis=1), cot_v[at, :])
         return carry
 
+    g_acc[...] = jnp.zeros_like(g_acc)
     lax.fori_loop(0, nch, two_chunk, 0)
-    scatter_nodes(gb, rb, dot(cot_t[...], mn[...]).T, 3)
+    scatter_nodes(gb, rb, g_acc[...], 3)
 
     loads[3].wait()
     bias_two = b2[...]
@@ -362,17 +381,22 @@
         def _():
             drain(ft.at[pl.ds(0, fd), pl.ds(0, rows)], fedge.at[h])
 
-    for m in range(2 * nch):
-        some = at_cols(0, 0, 0)
-        drain(some, psend.at[m])
-
-        @pl.when(jnp.logical_or(bound_next, bound_prev))
-        def _():
-            drain(some, pbound.at[m])
-
-        @pl.when(jnp.logical_not(skip))
-        def _():
-            drain(some, pfsend.at[m])
+    for h in range(2):
+        for c in range(nch + h):
+            m = h * nch + c
+            some = at_cols(0, *plan[h][c])
+            drain(some, psend.at[m])
+            if h == 1 and c == last:
+                drain(some, pbound.at[m])
+                continue
+
+            @pl.when(jnp.logical_or(bound_next, bound_prev))
+            def _():
+                drain(some, pbound.at[m])
+
+            @pl.when(jnp.logical_not(skip))
+            def _():
+                drain(some, pfsend.at[m])
 
     gather_nodes(qb, 1, 3)
     top = finish(0, 0)
@@ -438,8 +462,9 @@
             pltpu.VMEM((nf, rp, hid), F32),
             pltpu.VMEM((2 * hid, hid), BF),
             pltpu.VMEM((nn, 8, hid), F32),
+            pltpu.VMEM((hid, hid), F32),
             dma((7,)), dma((1,)), dma((nf,)), dma((2,)), dma((2,)), dma((2,)),
-            dma((2 * nch,)), dma((2 * nch,)), dma((2 * nch,)), dma((2 * nch,)), dma((2 * nch,)),
+            dma((2 * nch + 1,)), dma((2 * nch + 1,)), dma((2 * nch + 1,)), dma((2 * nch + 1,)), dma((2 * nch + 1,)),
             dma((7,)), dma((7,)), dma((nch,)),
         ],
         compiler_params=pltpu.CompilerParams(

time: 72.7 us -> 72.7 us (level)
  no operation moved by 1% of the time
where the time goes in v6:
time: 72.7 us; the launch traced here: 72.5 us
  Pallas kernels  71.9 us (99%)
    pallas_call x1, Pallas kernels, per_device(): pl.pallas_call(functools.partial(kernel, nn, nf, nb, neigh, ch), out_shap...  69.4 us
    pallas_call x1, Pallas kernels, per_device(): pl.pallas_call(hand_over, out_shape=(jax.ShapeDtypeStruct((rows, hid), BF...  2.51 us

profile of v6, /device:TPU:1, one launch (start us, length us, event | category | flops | bytes accessed | tf_op | source)
XLA Modules:
  0.0 72.5 jit_solution(258346504960950958)
XLA Ops:
  0.6 69.4 %sage.1 = (bf16[2048,256]{1,0:T(8,128)(2,1)}, bf16[512,256]{1,0:T(8,128)(2,1)}, f32[16,8,256]{2,1,0:T(8,128)}) custom-call(bf16[16,16384]{1,0:T(8,128)(2,1)} %feats.1, s32[16,20]{1,0:T(8,128)} %src.1, bf16[16,20,128,128]{3,2,1,0:T(8,128)(2,1)} %a_hbm.1, bf16[128,512]{1,0:T(8,128)(2,1)} %w1_hbm.1, f32[1,256]{1,0:T(1,128)} %bitcast.3, ...), custom_call_target="tpu_custom_call" | custom-call | tf_op jit(solution)/shard_map/sage/pallas_call | solution.py:434
  70.0 2.5 %hand_over.1 = (bf16[2048,256]{1,0:T(8,128)(2,1)}, f32[512,256]{1,0:T(8,128)}, f32[1,256]{1,0:T(1,128)}) custom-call(bf16[2048,256]{1,0:T(8,128)(2,1)} %get-tuple-element.9.out, bf16[512,256]{1,0:T(8,128)(2,1)} %get-tuple-element.10.gw, f32[16,8,256]{2,1,0:T(8,128)} %get-tuple-element.11.gb), custom_call_target="tpu_custom_call" | custom-call | tf_op jit(solution)/shard_map/hand_over/pallas_call | solution.py:474

commit v7 on v6

--- a/solution.py
+++ b/solution.py
@@ -44,8 +44,8 @@
            feats, src, a_hbm, w1_hbm, b1, w2_hbm, b2, cot_hbm,
            out_hbm, gw_hbm, gb_hbm,
            ft, zb, fa, fb, a_v, pt, hn, mn, cot_v, cot_t, w1_v, w2_v, out_v,
-           gt, rt, qt, gb, rb, qb, gfin, bslot, g_acc,
-           load_sem, zsend, zrecv, fsend, fedge, frecv, psend, pbound, pfsend, pdir, pfwd,
+           gt, rt, qt, gb, rb, qb, gfin, bslot, g_acc, loc,
+           load_sem, zsend, zrecv, fsend, fedge, fextra, frecv, psend, pbound, pfsend, pdir, pfwd,
            ars, arr, out_sem):
     fd = feats.shape[0]
     rows = nb * TILE
@@ -56,7 +56,7 @@
     cr = ch * TILE
     plan = ([(c * ch, ch) for c in range(nch)],
             [(c * ch, ch) for c in range(nch - 1)] + [(nb - ch, ch // 2), (nb - ch // 2, ch // 2)])
-    last = nch
+    straight_set = ((1, nch),)
     n = lax.axis_index("nodes")
     f = lax.axis_index("feat")
     z = lax.rem(f, 2)
@@ -107,6 +107,8 @@
         j = lax.rem(partner + t, nf)
         remote(feats.at[:, columns(j)], zb.at[:, columns(j)], zsend.at[0], zrecv.at[t], n, partner).start()
 
+    cross = lax.rem(n + f, 2) == 1
+
     def spread(t, source, row, h):
         j = lax.rem(f + t, nf)
         s = source.at[:, columns(j)]
@@ -116,37 +118,32 @@
 
         def keep(part):
             pltpu.make_async_copy(s, to(part), frecv.at[h]).start()
+
+        def send(part, node, feat):
+            remote(s, to(part), fsend.at[h], frecv.at[h], node, feat).start()
+
+        def over(part, node, feat, sem, recv):
+            remote(s, to(part), sem, frecv.at[recv], node, jnp.int32(feat)).start()
 
         if t % 2 == 0:
             if t == 0:
                 keep(1)
             else:
-                remote(s, to(1), fsend.at[h], frecv.at[h], n, j).start()
+                send(1, n, j)
+            if h == 0:
+                pl.when(jnp.logical_and(j == nf - 1, lax.rem(n, 2) == 1))(
+                    lambda: over(0, n_next, 0, fextra.at[0], 1))
+                pl.when(jnp.logical_and(j == 0, lax.rem(n, 2) == 0))(
+                    lambda: over(2, n_prev, nf - 1, fextra.at[0], 1))
             return
-        dn = jnp.where(j == nf - 1, n_next, n)
-        df = lax.rem(j + 1, nf)
-        if t == nf - 1:
-            @pl.when(f == 0)
-            def _():
-                remote(s, to(0), fedge.at[h], frecv.at[h], dn, df).start()
-
-            @pl.when(f != 0)
-            def _():
-                keep(0)
-        else:
-            remote(s, to(0), fsend.at[h], frecv.at[h], dn, df).start()
-        dn = jnp.where(j == 0, n_prev, n)
-        df = lax.rem(j + nf - 1, nf)
-        if t == 1:
-            @pl.when(f == nf - 1)
-            def _():
-                remote(s, to(2), fedge.at[h], frecv.at[h], dn, df).start()
-
-            @pl.when(f != nf - 1)
-            def _():
-                keep(2)
-        else:
-            remote(s, to(2), fsend.at[h], frecv.at[h], dn, df).start()
+        ours = True if h == 0 else jnp.logical_not(cross)
+        for part, at_edge, step, node, feat, own in ((0, j == nf - 1, 1, n_next, 0, nf - 1),
+                                                     (2, j == 0, nf - 1, n_prev, nf - 1, 1)):
+            pl.when(jnp.logical_and(at_edge, ours))(
+                functools.partial(over, part, node, feat, fedge.at[h], h))
+            inside = functools.partial(keep, part) if t == own else functools.partial(
+                send, part, n, lax.rem(j + step, nf))
+            pl.when(jnp.logical_not(at_edge))(inside)
 
     for t in far_first:
         spread(t, feats, row_own, 0)
@@ -172,11 +169,16 @@
     first = (n * nf + f - 1) * nb
     total = nn * nf * nb
 
+    def locate(b, carry):
+        for k in range(neigh):
+            s = src[b, k] - first
+            s = jnp.where(s >= total, s - total, s)
+            s = jnp.where(s < 0, s + total, s)
+            loc[b, k] = jnp.minimum(s, 3 * nb - 1)
+        return carry
+
     def pick(table, b, k):
-        s = src[b, k] - first
-        s = jnp.where(s >= total, s - total, s)
-        s = jnp.where(s < 0, s + total, s)
-        return table[jnp.minimum(s, 3 * nb - 1)]
+        return table[loc[b, k]]
 
     def pair(b, k):
         return jnp.concatenate([a_v[b, k], a_v[b, k + 1]], axis=1)
@@ -203,7 +205,7 @@
     direct_n = jnp.where(f == 0, n_prev, jnp.where(f == nf - 1, n_next, n))
     direct_base = (2 - 2 * z) * nb
 
-    def one_chunk(table, row, h, m, block, count):
+    def one_chunk(table, row, h, m, block, count, straight=False):
         for i in range(count):
             b = block + i
             acc = None
@@ -219,12 +221,10 @@
             remote(own, at_cols(row, direct_base + block, count), pbound.at[m], pfwd.at[m],
                    direct_n, direct_f).start()
 
-        if h == 1 and count < ch:
-            if block == nb - count:
-                direct()
-                return
-
-        pl.when(jnp.logical_or(bound_next, bound_prev))(direct)
+        if straight:
+            direct()
+        else:
+            pl.when(jnp.logical_or(bound_next, bound_prev))(direct)
 
     skip = jnp.logical_or(jnp.logical_and(f == nf - 2, lax.rem(n, 2) == 1),
                           jnp.logical_and(f == 1, lax.rem(n, 2) == 0))
@@ -237,22 +237,23 @@
         row = (1 - z) * half if h == 0 else z * half
         came = at_cols(row, in_base + block, count)
         drain(came, pdir.at[m])
-        if h == 1 and c == last:
+        if (h, c) in straight_set:
             return
 
         @pl.when(jnp.logical_not(skip))
         def _():
             remote(came, at_cols(row, out_base + block, count), pfsend.at[m], pfwd.at[m], fwd_n, fwd_f).start()
 
+    lax.fori_loop(0, nb, locate, 0)
     arrange(fa, z * half, 0)
     loads[2].wait()
-    one_chunk(fa, z * half, 0, 0, 0, ch)
+    one_chunk(fa, z * half, 0, 0, 0, ch, (0, 0) in straight_set)
     pass_on(far_first[-2])
     if nch > 1:
-        one_chunk(fa, z * half, 0, 1, ch, ch)
+        one_chunk(fa, z * half, 0, 1, ch, ch, (0, 1) in straight_set)
     pass_on(far_first[-1])
     if nch > 2:
-        lax.fori_loop(2, nch, lambda c, u: (one_chunk(fa, z * half, 0, c, c * ch, ch), u)[1], 0)
+        lax.fori_loop(2, nch, lambda c, u: (one_chunk(fa, z * half, 0, c, c * ch, ch, (0, 2) in straight_set), u)[1], 0)
     arrange(fb, (1 - z) * half, 1)
     for c in range(nch):
         forward(0, c)
@@ -260,7 +261,7 @@
     if nch > 1:
         lax.fori_loop(0, nch - 1, lambda c, u: (one_chunk(fb, (1 - z) * half, 1, nch + c, c * ch, ch), u)[1], 0)
     for c in (nch - 1, nch):
-        one_chunk(fb, (1 - z) * half, 1, nch + c, *plan[1][c])
+        one_chunk(fb, (1 - z) * half, 1, nch + c, *plan[1][c], (1, c) in straight_set)
 
     loads[0].wait()
     order = [g * fd for g in range(0, nf, 2)] + [g * fd for g in range(1, nf, 2)]
@@ -276,11 +277,13 @@
             hn[at] = jnp.maximum(v, 0.0).astype(BF).reshape(2, TILE, hid)
             return carry
 
-        lax.fori_loop(0, count // 2, step, 0)
-
-    def scatter_nodes(g, r, grad, k):
+        lax.fori_loop(0, count // 2, step, 0, unroll=min(4, count // 2))
+
+    def pieces(g, grad):
         for i in range(nn):
             g[i] = grad[i * rp:(i + 1) * rp, :].astype(BF)
+
+    def scatter_nodes(g, r, k):
         for d in range(1, nn):
             dn = lax.rem(n + d, nn)
             remote(g.at[dn], r.at[n], ars.at[k], arr.at[k], dn, f).start()
@@ -305,17 +308,13 @@
         at = pl.ds(pl.multiple_of(half * hid + n * rp, rp), rp)
         gfin[at, :] = tot[0:rp, :].astype(BF)
         for d in range(1, nn):
-            remote(gfin.at[at], gfin.at[at], ars.at[k + 2], arr.at[k + 2], lax.rem(n + d, nn), f).start()
+            remote(gfin.at[at], gw_hbm.at[at], ars.at[k + 2], arr.at[k + 2], lax.rem(n + d, nn), f).start()
+        pltpu.make_async_copy(gfin.at[at], gw_hbm.at[at], load_sem.at[4 + half]).start()
         if half == 0:
             bslot[n] = tot[rp:, :]
             for d in range(1, nn):
-                remote(bslot.at[n], bslot.at[n], ars.at[6], arr.at[6], lax.rem(n + d, nn), f).start()
-
-    def finish(half, k):
-        some = gfin.at[pl.ds(half * hid, (nn - 1) * rp)]
-        drain(some, arr.at[k + 2])
-        at = pl.ds(half * hid, hid)
-        return pltpu.make_async_copy(gfin.at[at], gw_hbm.at[at], load_sem.at[4 + half])
+                remote(bslot.at[n], gb_hbm.at[n], ars.at[6], arr.at[6], lax.rem(n + d, nn), f).start()
+            pltpu.make_async_copy(bslot.at[n], gb_hbm.at[n], load_sem.at[6]).start()
 
     def halo(c):
         block, count = plan[1][c]
@@ -324,18 +323,22 @@
         drain(at_cols(0, block, count), pfwd.at[nch + c])
         hidden(out_base + block, count)
 
+    forward(1, 0)
     hidden(nb, nb)
-    for c in range(min(2, nch)):
+    forward(1, 1)
+    pieces(gt, dot(cot_t[...], hn[nb:2 * nb].reshape(rows, hid)).T)
+    for c in range(2, nch):
         forward(1, c)
-    scatter_nodes(gt, rt, dot(cot_t[...], hn[nb:2 * nb].reshape(rows, hid)).T, 0)
-    for c in range(2, nch + 1):
-        forward(1, c)
-    hidden(in_base, nb)
-    for c in range(nch - 1):
+        if c == 2:
+            hidden(in_base, nb // 2)
+    scatter_nodes(gt, rt, 0)
+    forward(1, nch)
+    if nch > 2:
+        hidden(in_base + nb // 2, nb // 2)
+    else:
+        hidden(in_base, nb)
+    for c in range(nch + 1):
         halo(c)
-    share_feat(gt, rt, qt, 0, bias_part)
-    halo(nch - 1)
-    halo(nch)
 
     def two_chunk(c, carry):
         turned = []
@@ -354,8 +357,11 @@
         return carry
 
     g_acc[...] = jnp.zeros_like(g_acc)
-    lax.fori_loop(0, nch, two_chunk, 0)
-    scatter_nodes(gb, rb, g_acc[...], 3)
+    lax.fori_loop(0, nch - 1, two_chunk, 0)
+    share_feat(gt, rt, qt, 0, bias_part)
+    two_chunk(nch - 1, 0)
+    pieces(gb, g_acc[...])
+    scatter_nodes(gb, rb, 3)
 
     loads[3].wait()
     bias_two = b2[...]
@@ -374,19 +380,30 @@
     share_feat(gb, rb, qb, 3, None)
 
     drain(zb, zsend.at[0])
+    piece = ft.at[pl.ds(0, fd), pl.ds(0, rows)]
+    ends = jnp.logical_or(f == 0, f == nf - 1)
     for h in range(2):
-        drain(ft.at[pl.ds(0, (nf + 1) * fd // 3), :], fsend.at[h])
-
-        @pl.when(jnp.logical_or(f == 0, f == nf - 1))
+        @pl.when(ends)
         def _():
-            drain(ft.at[pl.ds(0, fd), pl.ds(0, rows)], fedge.at[h])
+            drain(ft.at[pl.ds(0, (nf + 1) * fd // 3), :], fsend.at[h])
+
+        @pl.when(jnp.logical_not(ends))
+        def _():
+            drain(zb, fsend.at[h])
+
+    drain(piece, fedge.at[0])
+
+    @pl.when(jnp.logical_not(cross))
+    def _():
+        drain(piece, fedge.at[1])
+        drain(piece, fextra.at[0])
 
     for h in range(2):
         for c in range(nch + h):
             m = h * nch + c
             some = at_cols(0, *plan[h][c])
             drain(some, psend.at[m])
-            if h == 1 and c == last:
+            if (h, c) in straight_set:
                 drain(some, pbound.at[m])
                 continue
 
@@ -399,11 +416,8 @@
                 drain(some, pfsend.at[m])
 
     gather_nodes(qb, 1, 3)
-    top = finish(0, 0)
-    top.start()
-    drain(bslot.at[pl.ds(0, nn - 1)], arr.at[6])
-    bias = pltpu.make_async_copy(bslot, gb_hbm, load_sem.at[6])
-    bias.start()
+    drain(gw_hbm.at[pl.ds(0, (nn - 1) * rp)], arr.at[2])
+    drain(gb_hbm.at[pl.ds(0, nn - 1)], arr.at[6])
     for k, (g, q) in ((0, (gt, qt)), (3, (gb, qb))):
         drain(g.at[pl.ds(0, nn - 1)], ars.at[k])
         drain(q.at[pl.ds(0, nf - 1)], ars.at[k + 1])
@@ -411,11 +425,11 @@
     drain(bslot.at[pl.ds(0, nn - 1)], ars.at[6])
     for c in range(nch):
         drain(out_v.at[pl.ds(c * cr, cr)], out_sem.at[c])
-    bottom = finish(1, 3)
-    bottom.start()
-    top.wait()
-    bias.wait()
-    bottom.wait()
+    mine = gfin.at[pl.ds(0, rp)]
+    drain(mine, load_sem.at[4])
+    drain(bslot.at[0], load_sem.at[6])
+    drain(mine, load_sem.at[5])
+    drain(gw_hbm.at[pl.ds(0, (nn - 1) * rp)], arr.at[5])
 
 
 def per_device(nn, nf, feats, tile_src, tile_weight, w_one, b_one, w_two, b_two, cotangent):
@@ -463,7 +477,8 @@
             pltpu.VMEM((2 * hid, hid), BF),
             pltpu.VMEM((nn, 8, hid), F32),
             pltpu.VMEM((hid, hid), F32),
-            dma((7,)), dma((1,)), dma((nf,)), dma((2,)), dma((2,)), dma((2,)),
+            pltpu.SMEM((nb, neigh), jnp.int32),
+            dma((7,)), dma((1,)), dma((nf,)), dma((2,)), dma((2,)), dma((1,)), dma((2,)),
             dma((2 * nch + 1,)), dma((2 * nch + 1,)), dma((2 * nch + 1,)), dma((2 * nch + 1,)), dma((2 * nch + 1,)),
             dma((7,)), dma((7,)), dma((nch,)),
         ],

time: 72.7 us -> 70 us (0.963)
  Pallas kernels: 71.9 us -> 69.2 us
    pallas_call x1, Pallas kernels: 69.4 us -> 66.7 us  [per_device(): pl.pallas_call(functools.partial(kernel, nn, nf, nb, neigh, ch), out_shap...]
where the time goes in v7:
time: 70 us; the launch traced here: 69.8 us
  Pallas kernels  69.2 us (99%)
    pallas_call x1, Pallas kernels, per_device(): pl.pallas_call(functools.partial(kernel, nn, nf, nb, neigh, ch), out_shap...  66.7 us
    pallas_call x1, Pallas kernels, per_device(): pl.pallas_call(hand_over, out_shape=(jax.ShapeDtypeStruct((rows, hid), BF...  2.51 us

profile of v7, /device:TPU:1, one launch (start us, length us, event | category | flops | bytes accessed | tf_op | source)
XLA Modules:
  0.0 69.8 jit_solution(10234379657291633590)
XLA Ops:
  0.6 66.7 %sage.1 = (bf16[2048,256]{1,0:T(8,128)(2,1)}, bf16[512,256]{1,0:T(8,128)(2,1)}, f32[16,8,256]{2,1,0:T(8,128)}) custom-call(bf16[16,16384]{1,0:T(8,128)(2,1)} %feats.1, s32[16,20]{1,0:T(8,128)} %src.1, bf16[16,20,128,128]{3,2,1,0:T(8,128)(2,1)} %a_hbm.1, bf16[128,512]{1,0:T(8,128)(2,1)} %w1_hbm.1, f32[1,256]{1,0:T(1,128)} %bitcast.3, ...), custom_call_target="tpu_custom_call" | custom-call | tf_op jit(solution)/shard_map/sage/pallas_call | solution.py:448
  67.3 2.5 %hand_over.1 = (bf16[2048,256]{1,0:T(8,128)(2,1)}, f32[512,256]{1,0:T(8,128)}, f32[1,256]{1,0:T(1,128)}) custom-call(bf16[2048,256]{1,0:T(8,128)(2,1)} %get-tuple-element.9.out, bf16[512,256]{1,0:T(8,128)(2,1)} %get-tuple-element.10.gw, f32[16,8,256]{2,1,0:T(8,128)} %get-tuple-element.11.gb), custom_call_target="tpu_custom_call" | custom-call | tf_op jit(solution)/shard_map/hand_over/pallas_call | solution.py:489

commit v8 on v7

--- a/solution.py
+++ b/solution.py
@@ -31,13 +31,32 @@
     return lax.dot_general(a, b, (((1,), (1,)), ((), ())), preferred_element_type=F32)
 
 
-def hand_over(out, gw, gb, out_copy, gw_wide, gb_sum):
-    out_copy[...] = out[...]
-    gw_wide[...] = gw[...].astype(F32)
-    tot = gb[0]
+def hand_over(out, gw, gb, out_copy, gw_wide, gb_sum, out_v, gw_v, gb_v, wide_v, sum_v, came, left):
+    parts = came.shape[0] - 2
+    size = out.shape[0] // parts
+    here = [pltpu.make_async_copy(out.at[pl.ds(i * size, size)], out_v.at[pl.ds(i * size, size)], came.at[i])
+            for i in range(parts)]
+    there = [pltpu.make_async_copy(out_v.at[pl.ds(i * size, size)], out_copy.at[pl.ds(i * size, size)], left.at[i])
+             for i in range(parts)]
+    here += [pltpu.make_async_copy(gw, gw_v, came.at[parts]), pltpu.make_async_copy(gb, gb_v, came.at[parts + 1])]
+    there += [pltpu.make_async_copy(wide_v, gw_wide, left.at[parts]),
+              pltpu.make_async_copy(sum_v, gb_sum, left.at[parts + 1])]
+    for i in (parts, *range(parts), parts + 1):
+        here[i].start()
+    here[parts].wait()
+    wide_v[...] = gw_v[...].astype(F32)
+    there[parts].start()
+    for i in range(parts):
+        here[i].wait()
+        there[i].start()
+    here[parts + 1].wait()
+    tot = gb_v[0]
     for i in range(1, gb.shape[0]):
-        tot = tot + gb[i]
-    gb_sum[...] = jnp.sum(tot, axis=0, keepdims=True)
+        tot = tot + gb_v[i]
+    sum_v[...] = jnp.sum(tot, axis=0, keepdims=True)
+    there[parts + 1].start()
+    for copy in there:
+        copy.wait()
 
 
 def kernel(nn, nf, nb, neigh, chunk_blocks,
@@ -54,9 +73,13 @@
     ch = chunk_blocks
     nch = nb // ch
     cr = ch * TILE
-    plan = ([(c * ch, ch) for c in range(nch)],
-            [(c * ch, ch) for c in range(nch - 1)] + [(nb - ch, ch // 2), (nb - ch // 2, ch // 2)])
-    straight_set = ((1, nch),)
+    hc = ch // 2
+    start = [(0, hc), (hc, hc)]
+    plan = (start + [(c * ch, ch) for c in range(1, nch)],
+            start + [(c * ch, ch) for c in range(1, nch - 1)] + [(nb - ch, hc), (nb - hc, hc)])
+    first_b = len(plan[0])
+    last = len(plan[1]) - 1
+    straight_set = ((1, last),)
     n = lax.axis_index("nodes")
     f = lax.axis_index("feat")
     z = lax.rem(f, 2)
@@ -232,7 +255,7 @@
     fwd_n = jnp.where(f == nf - 2, n_next, jnp.where(f == 1, n_prev, n))
 
     def forward(h, c):
-        m = h * nch + c
+        m = h * first_b + c
         block, count = plan[h][c]
         row = (1 - z) * half if h == 0 else z * half
         came = at_cols(row, in_base + block, count)
@@ -247,21 +270,21 @@
     lax.fori_loop(0, nb, locate, 0)
     arrange(fa, z * half, 0)
     loads[2].wait()
-    one_chunk(fa, z * half, 0, 0, 0, ch, (0, 0) in straight_set)
+    row_a, row_b = z * half, (1 - z) * half
+    one_chunk(fa, row_a, 0, 0, *plan[0][0])
     pass_on(far_first[-2])
-    if nch > 1:
-        one_chunk(fa, z * half, 0, 1, ch, ch, (0, 1) in straight_set)
+    one_chunk(fa, row_a, 0, 1, *plan[0][1])
     pass_on(far_first[-1])
+    lax.fori_loop(1, nch, lambda c, u: (one_chunk(fa, row_a, 0, 1 + c, c * ch, ch), u)[1], 0)
+    arrange(fb, row_b, 1)
+    for c in range(first_b):
+        forward(0, c)
+    for c in range(2):
+        one_chunk(fb, row_b, 1, first_b + c, *plan[1][c])
     if nch > 2:
-        lax.fori_loop(2, nch, lambda c, u: (one_chunk(fa, z * half, 0, c, c * ch, ch, (0, 2) in straight_set), u)[1], 0)
-    arrange(fb, (1 - z) * half, 1)
-    for c in range(nch):
-        forward(0, c)
-
-    if nch > 1:
-        lax.fori_loop(0, nch - 1, lambda c, u: (one_chunk(fb, (1 - z) * half, 1, nch + c, c * ch, ch), u)[1], 0)
-    for c in (nch - 1, nch):
-        one_chunk(fb, (1 - z) * half, 1, nch + c, *plan[1][c], (1, c) in straight_set)
+        lax.fori_loop(1, nch - 1, lambda c, u: (one_chunk(fb, row_b, 1, first_b + 1 + c, c * ch, ch), u)[1], 0)
+    for c in (last - 1, last):
+        one_chunk(fb, row_b, 1, first_b + c, *plan[1][c], (1, c) in straight_set)
 
     loads[0].wait()
     order = [g * fd for g in range(0, nf, 2)] + [g * fd for g in range(1, nf, 2)]
@@ -316,29 +339,32 @@
                 remote(bslot.at[n], gb_hbm.at[n], ars.at[6], arr.at[6], lax.rem(n + d, nn), f).start()
             pltpu.make_async_copy(bslot.at[n], gb_hbm.at[n], load_sem.at[6]).start()
 
-    def halo(c):
+    def halo(c, seen):
         block, count = plan[1][c]
-        if c < nch:
-            drain(at_cols(0, *plan[0][c]), pfwd.at[c])
-        drain(at_cols(0, block, count), pfwd.at[nch + c])
+        for m in range(seen, first_b):
+            if plan[0][m][0] < block + count:
+                drain(at_cols(0, *plan[0][m]), pfwd.at[m])
+                seen = m + 1
+        drain(at_cols(0, block, count), pfwd.at[first_b + c])
         hidden(out_base + block, count)
+        return seen
 
     forward(1, 0)
+    forward(1, 1)
     hidden(nb, nb)
-    forward(1, 1)
+    if last > 3:
+        forward(1, 2)
     pieces(gt, dot(cot_t[...], hn[nb:2 * nb].reshape(rows, hid)).T)
-    for c in range(2, nch):
+    for c in range(3 if last > 3 else 2, last - 1):
         forward(1, c)
-        if c == 2:
-            hidden(in_base, nb // 2)
+    hidden(in_base, nb // 2)
+    forward(1, last - 1)
     scatter_nodes(gt, rt, 0)
-    forward(1, nch)
-    if nch > 2:
-        hidden(in_base + nb // 2, nb // 2)
-    else:
-        hidden(in_base, nb)
-    for c in range(nch + 1):
-        halo(c)
+    forward(1, last)
+    hidden(in_base + nb // 2, nb // 2)
+    seen = 0
+    for c in range(last + 1):
+        seen = halo(c, seen)
 
     def two_chunk(c, carry):
         turned = []
@@ -375,9 +401,9 @@
         return carry
 
     lax.fori_loop(0, nch, out_chunk, 0)
+
+    share_feat(gb, rb, qb, 3, None)
     gather_nodes(qt, 0, 0)
-
-    share_feat(gb, rb, qb, 3, None)
 
     drain(zb, zsend.at[0])
     piece = ft.at[pl.ds(0, fd), pl.ds(0, rows)]
@@ -399,8 +425,8 @@
         drain(piece, fextra.at[0])
 
     for h in range(2):
-        for c in range(nch + h):
-            m = h * nch + c
+        for c in range(len(plan[h])):
+            m = h * first_b + c
             some = at_cols(0, *plan[h][c])
             drain(some, psend.at[m])
             if (h, c) in straight_set:
@@ -479,7 +505,7 @@
             pltpu.VMEM((hid, hid), F32),
             pltpu.SMEM((nb, neigh), jnp.int32),
             dma((7,)), dma((1,)), dma((nf,)), dma((2,)), dma((2,)), dma((1,)), dma((2,)),
-            dma((2 * nch + 1,)), dma((2 * nch + 1,)), dma((2 * nch + 1,)), dma((2 * nch + 1,)), dma((2 * nch + 1,)),
+            dma((2 * nch + 3,)), dma((2 * nch + 3,)), dma((2 * nch + 3,)), dma((2 * nch + 3,)), dma((2 * nch + 3,)),
             dma((7,)), dma((7,)), dma((nch,)),
         ],
         compiler_params=pltpu.CompilerParams(
@@ -493,8 +519,16 @@
             jax.ShapeDtypeStruct((2 * hid, hid), F32),
             jax.ShapeDtypeStruct((1, hid), F32),
         ),
-        in_specs=[vm] * 3,
-        out_specs=(vm,) * 3,
+        in_specs=[anyspace] * 3,
+        out_specs=(anyspace,) * 3,
+        scratch_shapes=[
+            pltpu.VMEM((rows, hid), BF),
+            pltpu.VMEM((2 * hid, hid), BF),
+            pltpu.VMEM((nn, 8, hid), F32),
+            pltpu.VMEM((2 * hid, hid), F32),
+            pltpu.VMEM((1, hid), F32),
+            dma((4,)), dma((4,)),
+        ],
         name="hand_over",
     )(out, gw, gb)
     return out, gw, gb.reshape(hid)

time: 70 us -> 69.6 us (level)
  no operation moved by 1% of the time
where the time goes in v8:
time: 69.6 us; the launch traced here: 69.5 us
  Pallas kernels  68.8 us (99%)
    pallas_call x1, Pallas kernels, per_device(): pl.pallas_call(functools.partial(kernel, nn, nf, nb, neigh, ch), out_shap...  66.6 us
    pallas_call x1, Pallas kernels, per_device(): pl.pallas_call(hand_over, out_shape=(jax.ShapeDtypeStruct((rows, hid), BF...  2.2 us

profile of v8, /device:TPU:1, one launch (start us, length us, event | category | flops | bytes accessed | tf_op | source)
XLA Modules:
  0.0 69.5 jit_solution(3559139999181049481)
XLA Ops:
  0.6 66.6 %sage.1 = (bf16[2048,256]{1,0:T(8,128)(2,1)}, bf16[512,256]{1,0:T(8,128)(2,1)}, f32[16,8,256]{2,1,0:T(8,128)}) custom-call(bf16[16,16384]{1,0:T(8,128)(2,1)} %feats.1, s32[16,20]{1,0:T(8,128)} %src.1, bf16[16,20,128,128]{3,2,1,0:T(8,128)(2,1)} %a_hbm.1, bf16[128,512]{1,0:T(8,128)(2,1)} %w1_hbm.1, f32[1,256]{1,0:T(1,128)} %bitcast.3, ...), custom_call_target="tpu_custom_call" | custom-call | tf_op jit(solution)/shard_map/sage/pallas_call | solution.py:474
  67.3 2.2 %hand_over.1 = (bf16[2048,256]{1,0:T(8,128)(2,1)}, f32[512,256]{1,0:T(8,128)}, f32[1,256]{1,0:T(1,128)}) custom-call(bf16[2048,256]{1,0:T(8,128)(2,1)} %get-tuple-element.9.out, bf16[512,256]{1,0:T(8,128)(2,1)} %get-tuple-element.10.gw, f32[16,8,256]{2,1,0:T(8,128)} %get-tuple-element.11.gb), custom_call_target="tpu_custom_call" | custom-call | tf_op jit(solution)/shard_map/hand_over/pallas_call | solution.py:515

commit v9 on v8

--- a/solution.py
+++ b/solution.py
@@ -383,11 +383,10 @@
         return carry
 
     g_acc[...] = jnp.zeros_like(g_acc)
-    lax.fori_loop(0, nch - 1, two_chunk, 0)
-    share_feat(gt, rt, qt, 0, bias_part)
-    two_chunk(nch - 1, 0)
+    lax.fori_loop(0, nch, two_chunk, 0, unroll=2)
     pieces(gb, g_acc[...])
     scatter_nodes(gb, rb, 3)
+    share_feat(gt, rt, qt, 0, bias_part)
 
     loads[3].wait()
     bias_two = b2[...]

time: 69.6 us -> 69.2 us (level)
  no operation moved by 1% of the time
where the time goes in v9:
time: 69.2 us; the launch traced here: 69 us
  Pallas kernels  68.4 us (99%)
    pallas_call x1, Pallas kernels, per_device(): pl.pallas_call(functools.partial(kernel, nn, nf, nb, neigh, ch), out_shap...  66.2 us
    pallas_call x1, Pallas kernels, per_device(): pl.pallas_call(hand_over, out_shape=(jax.ShapeDtypeStruct((rows, hid), BF...  2.2 us

profile of v9, /device:TPU:1, one launch (start us, length us, event | category | flops | bytes accessed | tf_op | source)
XLA Modules:
  0.0 69.0 jit_solution(1548911588070691102)
XLA Ops:
  0.6 66.2 %sage.1 = (bf16[2048,256]{1,0:T(8,128)(2,1)}, bf16[512,256]{1,0:T(8,128)(2,1)}, f32[16,8,256]{2,1,0:T(8,128)}) custom-call(bf16[16,16384]{1,0:T(8,128)(2,1)} %feats.1, s32[16,20]{1,0:T(8,128)} %src.1, bf16[16,20,128,128]{3,2,1,0:T(8,128)(2,1)} %a_hbm.1, bf16[128,512]{1,0:T(8,128)(2,1)} %w1_hbm.1, f32[1,256]{1,0:T(1,128)} %bitcast.3, ...), custom_call_target="tpu_custom_call" | custom-call | tf_op jit(solution)/shard_map/sage/pallas_call | solution.py:473
  66.8 2.2 %hand_over.1 = (bf16[2048,256]{1,0:T(8,128)(2,1)}, f32[512,256]{1,0:T(8,128)}, f32[1,256]{1,0:T(1,128)}) custom-call(bf16[2048,256]{1,0:T(8,128)(2,1)} %get-tuple-element.9.out, bf16[512,256]{1,0:T(8,128)(2,1)} %get-tuple-element.10.gw, f32[16,8,256]{2,1,0:T(8,128)} %get-tuple-element.11.gb), custom_call_target="tpu_custom_call" | custom-call | tf_op jit(solution)/shard_map/hand_over/pallas_call | solution.py:514
